TPU v7x, 256 devices: a whole 4x4x8 slice. The times are simulated.
256 devices in a mesh: seq: 64 (over x, z, core), tp: 4 (over y).
Axes of the slice: x: 4, y: 4, z: 8, core: 2. Of those that a mesh axis runs over, the one named last changes fastest.
Arguments:
- inputs: bfloat16 [32768, 6144], P('seq'), may hold values from -6 to 6
- proj_weight: bfloat16 [4, 6144, 1024], P(None, 'seq', 'tp'), may hold values from -0.078125 to 0.078125
- decay_codes: int32 [8], P('tp'), may hold values from 1 to 32768, as said below
- norm_gain: float32 [1024], P('tp'), may hold values from 0.1 to 1.9
- out_weight: bfloat16 [1024, 6144], P('seq', 'tp'), may hold values from -0.1875 to 0.1875
Outputs:
- mixed: bfloat16 [32768, 6144], P('seq', 'tp')
Inputs may be any that keep to these rules, and one draw needn't show every extreme that they name: `decay_codes`: each is a power of 8.
All inputs are finite; a program needn't handle non-finite values.
Results may differ from a plain program's by a relative error of at most 0.0052.
Values may be sent and summed in bfloat16 or wider, within the bound.
A program may use at most 64 MiB of HBM per device.

v0:
```python
import jax
import jax.numpy as jnp
from jax import lax
from jax.sharding import PartitionSpec as P

HEAD_DIM = 128


def shards(inputs, proj_weight, decay_codes, norm_gain, out_weight):
    high = lax.Precision.HIGHEST
    length = inputs.shape[0]
    local_width = proj_weight.shape[2]
    local_heads = local_width // HEAD_DIM
    columns = inputs
    proj = jnp.einsum(
        "tr,arh->ath",
        columns,
        lax.all_gather(proj_weight, "seq", axis=1, tiled=True),
        preferred_element_type=jnp.float32,
    )
    acts = jax.nn.silu(proj[:3]).astype(jnp.bfloat16)
    heads = acts.reshape(3, length, local_heads, HEAD_DIM).transpose(0, 2, 1, 3)
    query, keys, values = (heads[0], heads[1], heads[2])
    log_decay = jnp.log1p(-decay_codes.astype(jnp.float32) * 1e-06)
    pos = jnp.arange(length).astype(jnp.float32)
    diff = pos[:, None] - pos[None, :]
    weights = jnp.where(
        (diff >= 0)[None], jnp.exp(jnp.maximum(diff, 0.0)[None] * log_decay[:, None, None]), 0.0
    )
    into = jnp.exp((pos + 1.0)[None, :] * log_decay[:, None])
    tail = jnp.exp((length - 1.0 - pos)[None, :] * log_decay[:, None])
    scores = jnp.einsum("htd,hsd->hts", query, keys, preferred_element_type=jnp.float32) * weights
    probs = scores.astype(jnp.bfloat16)
    intra = jnp.einsum("hts,hsd->htd", probs, values, preferred_element_type=jnp.float32)
    keys_wide = keys.astype(jnp.float32)
    values_wide = values.astype(jnp.float32)
    local_state = jnp.einsum(
        "hsd,hse->hde", keys_wide * tail[:, :, None], values_wide, precision=high
    )
    here = lax.axis_index("seq").astype(jnp.float32)
    piece = lax.all_gather(local_state[None], "seq", axis=0, tiled=True)
    source = jnp.arange(piece.shape[0]).astype(jnp.float32)
    distance = here - 1.0 - source
    factor = jnp.where(
        (distance >= 0)[:, None],
        jnp.exp(jnp.maximum(distance, 0.0)[:, None] * length * log_decay[None, :]),
        0.0,
    )
    prior = jnp.einsum("mh,mhde->hde", factor, piece, precision=high)
    inter = jnp.einsum(
        "htd,hde->hte", query.astype(jnp.float32) * into[:, :, None], prior, precision=high
    )
    attended = intra + inter
    scale = lax.rsqrt(jnp.mean(attended * attended, axis=2, keepdims=True) + 1e-06)
    normed = (attended * scale).transpose(1, 0, 2).reshape(length, local_width)
    hidden = (normed * norm_gain[None, :] * jax.nn.sigmoid(proj[3])).astype(jnp.bfloat16)
    all_heads = lax.all_gather(hidden, "tp", axis=1, tiled=True)
    columns = all_heads
    mixed = jnp.dot(
        columns,
        lax.all_gather(out_weight, "seq", axis=0, tiled=True),
        preferred_element_type=jnp.float32,
    )
    return mixed.astype(jnp.bfloat16)


def solution(mesh):
    in_specs = (P("seq", None), P(None, "seq", "tp"), P("tp"), P("tp"), P("seq", "tp"))
    out_specs = P("seq", "tp")
    return jax.shard_map(shards, mesh=mesh, in_specs=in_specs, out_specs=out_specs, check_vma=False)
```

profile of v0, /device:TPU:1, one launch (start us, length us, event | category | flops | bytes accessed | tf_op | source)
XLA Modules:
  0.0 312.0 jit_solution(1368901122843580735)
XLA Ops:
  6.5 0.0 all-gather.6.cloned.1.call-start
  6.5 0.7 all-gather.6.cloned.1.call-update
  7.3 0.0 all-gather.12.cloned.1.call-start
  7.3 0.7 multiply_log-plus-one_fusion
  8.0 0.1 multiply_exponential_fusion.1
  8.1 96.3 %all-gather.6.cloned.1.call-done = bf16[4,6144,256]{2,1,0:T(8,128)(2,1)} async-done(((bf16[4,96,256]{2,1,0:T(8,128)(2,1)}), bf16[4,6144,256]{2,1,0:T(8,128)(2,1)}) %all-gather.6.cloned.1.call-update) | async-done | bytes 12582928 | tf_op jit(solution)/shard_map/all_gather | solution.py:18
  104.4 11.6 %fusion.2 = f32[4,512,256]{1,2,0:T(8,128)S(1)} fusion(bf16[4,6144,256]{2,1,0:T(8,128)(2,1)} %all-gather.6.cloned.1.call-done, bf16[512,6144]{1,0:T(8,128)(2,1)} %param.5), kind=kOutput, calls=%fused_computation.5 | convolution fusion | flops 6442450944 | bytes 20971520 | tf_op jit(solution)/shard_map/tr,arh->ath/dot_general | solution.py:15
  115.9 0.4 multiply_convert_fusion.1
  116.4 1.1 fusion.16
  117.4 0.0 all-gather.12.cloned.1.call-update
  117.4 0.0 all-gather.10.cloned.1.call-start
  117.5 0.7 all-gather.10.cloned.1.call-update
  118.2 0.0 all-gather.8.cloned.1.call-start
  118.3 0.1 select_bitcast_fusion
  118.4 0.9 subtract_compare_fusion
  119.3 1.1 subtract_maximum_fusion
  120.4 77.1 %all-gather.12.cloned.1.call-done = f32[128,128,128]{2,1,0:T(8,128)} async-done(((f32[2,128,128]{2,1,0:T(8,128)}), f32[128,128,128]{2,1,0:T(8,128)}) %all-gather.12.cloned.1.call-update) | async-done | bytes 8388624 | tf_op jit(solution)/shard_map/all_gather | solution.py:41
  197.5 4.0 %multiply_reduce_fusion = f32[2,128,128]{2,1,0:T(8,128)S(1)} fusion(f32[2,64,128,128]{3,2,0,1:T(8,128)} %bitcast.59, f32[2,64]{0,1:T(8,128)S(1)} %select_bitcast_fusion), kind=kLoop, calls=%fused_computation | loop fusion | flops 4161536 | bytes 8520192 | tf_op jit(solution)/shard_map/mh,mhde->hde/dot_general | solution.py:49
  201.5 0.6 fusion.19
  202.2 0.0 copy-start
  202.2 3.1 multiply_reduce_fusion.1
  205.3 1.1 bitcast_multiply_fusion.1
  206.4 0.0 copy-done
  206.4 0.9 fusion.22
  207.3 0.0 all-gather.8.cloned.1.call-update
  207.3 68.6 %all-gather.10.cloned.1.call-done = bf16[1024,1536]{1,0:T(8,128)(2,1)} async-done(((bf16[16,1536]{1,0:T(8,128)(2,1)}), bf16[1024,1536]{1,0:T(8,128)(2,1)}) %all-gather.10.cloned.1.call-update) | async-done | bytes 3145744 | tf_op jit(solution)/shard_map/all_gather | solution.py:61
  275.9 24.4 %all-gather.8.cloned.1.call-done = bf16[512,1024]{0,1:T(8,128)(2,1)} async-done(((bf16[512,256]{0,1:T(8,128)(2,1)}), bf16[512,1024]{0,1:T(8,128)(2,1)}) %all-gather.8.cloned.1.call-update) | async-done | bytes 1048592 | tf_op jit(solution)/shard_map/all_gather | solution.py:57
  300.3 5.2 %convolution_convert_fusion = bf16[512,1536]{1,0:T(8,128)(2,1)} fusion(bf16[512,1024]{0,1:T(8,128)(2,1)} %all-gather.8.cloned.1.call-done, bf16[1024,1536]{1,0:T(8,128)(2,1)} %all-gather.10.cloned.1.call-done), kind=kOutput, calls=%fused_computation.3 | convolution fusion | flops 1611399168 | bytes 5767168 | tf_op jit(solution)/shard_map/dot_general | solution.py:59
  (5 shorter events, 0.0 us)
Async XLA Ops:
  6.5 97.8 %all-gather.6.cloned.1.call-start = ((), (), s32[]{:S(2)}) async-start(), calls=%async_computation | async-start | bytes 12779520 | tf_op jit(solution)/shard_map/all_gather | solution.py:18
  7.3 190.2 %all-gather.12.cloned.1.call-start = ((), (), s32[]{:S(2)}) async-start(), calls=%async_computation.3 | async-start | bytes 8519680 | tf_op jit(solution)/shard_map/all_gather | solution.py:41
  117.4 158.4 %all-gather.10.cloned.1.call-start = ((), (), s32[]{:S(2)}) async-start(), calls=%async_computation.2 | async-start | bytes 3194880 | tf_op jit(solution)/shard_map/all_gather | solution.py:61
  118.2 182.1 %all-gather.8.cloned.1.call-start = ((), (), s32[]{:S(2)}) async-start(), calls=%async_computation.1 | async-start | bytes 1310720 | tf_op jit(solution)/shard_map/all_gather | solution.py:57
  202.2 4.2 %copy-start = (f32[256]{0:T(256)S(1)}, f32[256]{0:T(256)}, u32[]{:S(2)}) copy-start(f32[256]{0:T(256)} %param.8) | copy-start | bytes 3076
Sparse Core Ops, SparseCore 0:
  10.2 94.1 all-gather.5
  117.6 79.8 all-gather.11
  200.3 75.5 all-gather.9
  277.6 22.6 all-gather.7
where the time goes:
time: 312 us
  waiting for transfers between devices  268 us (86%)
  matrix products  21.5 us (7%)
  between operations  13.2 us (4%)
  other arithmetic  9.31 us (3%)
    all_gather x1, waiting for transfers between devices, shards(): lax.all_gather(proj_weight, 'seq', axis=1, tiled=True)  96.3 us
    all_gather x1, waiting for transfers between devices, shards(): piece = lax.all_gather(local_state[None], 'seq', axis=0, tiled=True)  77.1 us
    all_gather x1, waiting for transfers between devices, shards(): lax.all_gather(out_weight, 'seq', axis=0, tiled=True)  68.6 us
    all_gather x1, waiting for transfers between devices, shards(): all_heads = lax.all_gather(hidden, 'tp', axis=1, tiled=True)  24.4 us
    dot_general x1, matrix products, shards(): jnp.einsum('tr,arh->ath', columns, lax.all_gather(proj_weight, 'seq', axi...  11.6 us
  transfers between devices with their start and end apart: 4, of which 4 were waited for; matrix products, arithmetic and copies ran while one was open for 4% of the time, Pallas kernels for 0%

commit v1 on v0

v1 whole, which is shorter than its diff:
```python
import functools

import jax
import jax.numpy as jnp
from jax import lax
from jax.experimental import pallas as pl
from jax.experimental.pallas import tpu as pltpu
from jax.sharding import PartitionSpec as P

NX, NZ, NY = 4, 8, 4
T = 512
D = 6144
HD = 128
F = 256
SH = 96
KX = D // NX
MESH = pl.DeviceIdType.MESH
BF = jnp.bfloat16
F32 = jnp.float32

GROUPS = ((0, 2, 32), (2, 1, 32), (3, 1, 48), (4, 1, 48))
OFFSETS = (0, 3, 6, 9)
STAGES = 7
NSLOT = 40


def kernel(x_hbm, wp_hbm, codes, gain_ref, wo_hbm, out_hbm,
           buf, xv, wts, acc, kv, qv, att, hid, oacc, outv,
           state, sx, snd, rcv, stg, pri,
           load_sem, own_send, own_recv, recv, relay_recv, send_sem,
           st_send, st_recv, h_send, h_recv, out_sem):
    s = lax.axis_index("seq")
    y = lax.axis_index("tp")
    x, z, c = s // 16, (s // 2) % 8, s % 2
    q = s // 2

    def dev(px, pz, pc, py):
        return {"seq": (px * NZ + pz) * 2 + pc, "tp": py}

    xp, xm = (x + 1) % NX, (x + 3) % NX
    zp, zm = (z + 1) % NZ, (z + 7) % NZ
    yp, ym = (y + 1) % NY, (y + 3) % NY
    x2, z4, y2 = (x + 2) % NX, (z + 4) % NZ, (y + 2) % NY
    sib = dev(x, z, 1 - c, y)
    to = {"xp": dev(xp, z, c, y), "xm": dev(xm, z, c, y), "zp": dev(x, zp, c, y), "zm": dev(x, zm, c, y)}
    to_yp, to_ym = dev(x, z, c, yp), dev(x, z, c, ym)
    z_1 = z + 1 - 2 * (z % 2)
    z_2 = z + 2 - 4 * ((z // 2) % 2)
    x_1 = x + 1 - 2 * (x % 2)
    partners = (dev(x, z_1, c, y), dev(x, z_2, c, y), dev(x, z4, c, y), dev(x_1, z, c, y), dev(x2, z, c, y))

    x_load = pltpu.make_async_copy(x_hbm, xv, load_sem.at[0])
    x_load.start()
    loads = [
        [pltpu.make_async_copy(wp_hbm.at[pl.ds(1, 2)], buf.at[pl.ds(0, 2), x, z, c], load_sem.at[1])],
        [pltpu.make_async_copy(wp_hbm.at[pl.ds(0, 1)], buf.at[pl.ds(2, 1), x, z, c], load_sem.at[2])],
        [pltpu.make_async_copy(wp_hbm.at[pl.ds(3, 1)], buf.at[pl.ds(3, 1), x, z, c], load_sem.at[3])],
        [pltpu.make_async_copy(wo_hbm.at[:, pl.ds(F * j, F)], buf.at[4, x, z, c, pl.ds(16 * j, 16), :], load_sem.at[4 + j])
         for j in range(6)],
    ]
    for group in loads:
        for copy in group:
            copy.start()

    barrier = pltpu.get_barrier_semaphore()
    greet = list(to.values()) + [sib, to_yp, to_ym, partners[1], partners[2], partners[4]]
    for other in greet:
        pl.semaphore_signal(barrier, inc=1, device_id=other, device_id_type=MESH)
    pl.semaphore_wait(barrier, len(greet))

    def rcopy(src, dst, ssem, rsem, device):
        return pltpu.make_async_remote_copy(src, dst, ssem, rsem, device_id=device, device_id_type=MESH)

    def own_copy(g):
        i0, n, _ = GROUPS[g]
        ref = buf.at[pl.ds(i0, n), x, z, c]
        return rcopy(ref, ref, own_send.at[g], own_recv.at[g], sib)

    for g in range(len(GROUPS)):
        for copy in loads[g]:
            copy.wait()
        own_copy(g).start()

    pos = lambda shape, dim: lax.broadcasted_iota(jnp.int32, shape, dim).astype(F32)
    log_decay = [jnp.log1p(-(jnp.full((1, HD), codes[h], jnp.int32).astype(F32)) * 1e-06) for h in range(2)]
    ld_mine = jnp.where(c == 0, log_decay[0], log_decay[1])

    def table(r, carry):
        row = pos((64, T), 0) + (r * 64).astype(F32)
        diff = row - pos((64, T), 1)
        for h in range(2):
            ld = jnp.concatenate([log_decay[h]] * (T // HD), axis=1)
            w = jnp.where(diff >= 0, jnp.exp(jnp.maximum(diff, 0.0) * ld), 0.0)
            wts[h, pl.ds(pl.multiple_of(r * 64, 64), 64), :] = w
        return carry

    def piece(g, px, pz, rows, half=None):
        i0, n, _ = GROUPS[g]
        cc = pl.ds(0, 2) if half is None else pl.ds(half, 1)
        return buf.at[pl.ds(i0, n), px, pz, cc, pl.ds(*rows), :]

    def send(g, kind, ref, slot, where):
        rcopy(ref, ref, send_sem.at[g, kind], recv.at[g, slot], to[where]).start()

    def arrived(g, ref, slot):
        rcopy(ref, ref, send_sem.at[g, 0], recv.at[g, slot], sib).wait_recv()

    def relay(g, kind, ref):
        rcopy(ref, ref, send_sem.at[g, 2 + kind], relay_recv.at[g, kind], sib).start()

    def stage_a(g, t):
        i0, n, a = GROUPS[g]
        rows = (0, a)
        pc = functools.partial(piece, g, rows=rows)
        if t == 0:
            send(g, 0, pc(x, z), 0, "xp")
            send(g, 0, pc(x, z), 1, "xm")
        if t == 1:
            arrived(g, pc(xm, z), 0)
            send(g, 0, pc(xm, z, half=0), 2, "xp")
            arrived(g, pc(xp, z), 1)
            send(g, 0, pc(xp, z, half=1), 3, "xm")
        if t == 2:
            arrived(g, pc(x2, z, half=0), 2)
            arrived(g, pc(x2, z, half=1), 3)
        for k, (px, start) in reversed(list(enumerate(((x, 0), (xm, 1), (xp, 1), (x2, 2))))):
            h = t - start
            slot = lambda hop, way: 4 + (k * 4 + hop) * 2 + way
            down, up = (z + 8 - h) % NZ, (z + h) % NZ
            if h == 0:
                send(g, 1, pc(px, z), slot(0, 0), "zp")
                send(g, 1, pc(px, z), slot(0, 1), "zm")
            elif 1 <= h <= 3:
                arrived(g, pc(px, down), slot(h - 1, 0))
                send(g, 1, pc(px, down, half=None if h < 3 else 0), slot(h, 0), "zp")
                arrived(g, pc(px, up), slot(h - 1, 1))
                send(g, 1, pc(px, up, half=None if h < 3 else 1), slot(h, 1), "zm")
            elif h == 4:
                arrived(g, pc(px, z4, half=0), slot(3, 0))
                arrived(g, pc(px, z4, half=1), slot(3, 1))
        if t == 1:
            relay(g, 0, pc(xm, z))
            relay(g, 0, pc(xp, z))
        if t == 2:
            relay(g, 0, pc(x2, z))
        if t >= 3:
            h = t - 2
            line = lambda pz: buf.at[pl.ds(i0, n), :, pz, :, pl.ds(*rows), :]
            relay(g, 1, line((z + 8 - h) % NZ))
            if h < 4:
                relay(g, 1, line((z + h) % NZ))

    def stage_b(g, t):
        i0, n, a = GROUPS[g]
        rows = (a, SH - a)
        pc = functools.partial(piece, g, rows=rows)
        down, up = (z + 8 - t) % NZ, (z + t) % NZ
        if t == 0:
            send(g, 0, pc(x, z), 0, "zp")
            send(g, 0, pc(x, z), 1, "zm")
        elif t <= 3:
            arrived(g, pc(x, down), 2 * t - 2)
            send(g, 0, pc(x, down, half=None if t < 3 else 0), 2 * t, "zp")
            arrived(g, pc(x, up), 2 * t - 1)
            send(g, 0, pc(x, up, half=None if t < 3 else 1), 2 * t + 1, "zm")
        elif t == 4:
            arrived(g, pc(x, z4, half=0), 6)
            arrived(g, pc(x, z4, half=1), 7)
        chains = ((0, 0), (7, 1), (1, 1), (6, 2), (2, 2), (5, 3), (3, 3), (4, 4))
        for k, (dz, start) in reversed(list(enumerate(chains))):
            j = t - start
            pz = (z + dz) % NZ
            slot = 8 + 4 * k
            if j == 0:
                send(g, 1, pc(x, pz), slot, "xp")
                send(g, 1, pc(x, pz), slot + 1, "xm")
            elif j == 1:
                arrived(g, pc(xm, pz), slot)
                send(g, 1, pc(xm, pz, half=0), slot + 2, "xp")
                arrived(g, pc(xp, pz), slot + 1)
                send(g, 1, pc(xp, pz, half=1), slot + 3, "xm")
            elif j == 2:
                arrived(g, pc(x2, pz, half=0), slot + 2)
                arrived(g, pc(x2, pz, half=1), slot + 3)
        if 1 <= t <= 3:
            relay(g, 0, pc(x, down))
            relay(g, 0, pc(x, up))
        if t == 4:
            relay(g, 0, pc(x, z4))
        line = lambda px: buf.at[pl.ds(i0, n), px, :, :, pl.ds(*rows), :]
        if t == 5:
            relay(g, 1, line(xm))
            relay(g, 1, line(xp))
        if t == 6:
            relay(g, 1, line(x2))

    def stage(g, t):
        if t == 0:
            i0, n, _ = GROUPS[g]
            ref = buf.at[pl.ds(i0, n), x, z, 1 - c]
            rcopy(ref, ref, own_send.at[g], own_recv.at[g], sib).wait_recv()

        @pl.when(c == 0)
        def _():
            stage_a(g, t)

        @pl.when(c == 1)
        def _():
            stage_b(g, t)

    def sizes(g, core):
        i0, n, a = GROUPS[g]
        if core == 0:
            return [buf.at[pl.ds(i0, n), pl.ds(0, 3), 0, :, pl.ds(0, a), :],
                    buf.at[pl.ds(i0, n), :, pl.ds(0, 7), :, pl.ds(0, a), :]]
        return [buf.at[pl.ds(i0, n), 0, pl.ds(0, 7), :, pl.ds(a, SH - a), :],
                buf.at[pl.ds(i0, n), pl.ds(0, 3), :, :, pl.ds(a, SH - a), :]]

    def relays_arrived(g):
        for core in range(2):
            @pl.when(c == 1 - core)
            def _(core=core):
                for kind, ref in enumerate(sizes(g, core)):
                    rcopy(ref, ref, send_sem.at[g, 0], relay_recv.at[g, kind], sib).wait_recv()

    def sends_done(g):
        own_copy(g).wait_send()
        for core in range(2):
            @pl.when(c == core)
            def _(core=core):
                for kind, ref in enumerate(sizes(g, core)):
                    for w in (0, 2):
                        rcopy(ref, ref, send_sem.at[g, kind + w], relay_recv.at[g, 0], sib).wait_send()

    def project(item, xb):
        part = jnp.dot(xv[:, KX * xb:KX * (xb + 1)], buf[item, xb].reshape(KX, F), preferred_element_type=F32)
        if xb == 0:
            acc[...] = part
        else:
            acc[...] += part

    def silu(v):
        return v * jax.nn.sigmoid(v)

    def local_state():
        for h in range(2):
            tail = jnp.exp((T - 1.0 - pos((T, HD), 0)) * log_decay[h])
            cols = pl.ds(HD * h, HD)
            kt = (kv[0, :, cols].astype(F32) * tail).astype(BF)
            state[h] = lax.dot_general(kt, kv[1, :, cols], (((0,), (0,)), ((), ())), preferred_element_type=F32)

    whole = lambda n: jnp.exp((n * T) * ld_mine)
    total = {}

    def scan_open():
        rcopy(state.at[1 - c], sx, st_send.at[0], st_recv.at[0], sib).start()

    def scan_chip():
        rcopy(state.at[1 - c], sx, st_send.at[0], st_recv.at[0], sib).wait_recv()
        mine, other = state[c], sx[...]
        decay = whole(1.0)
        first = jnp.where(c == 0, mine, other)
        second = jnp.where(c == 0, other, mine)
        total["first"] = first
        stg[0] = first
        tot = decay * first + second
        stg[1] = tot
        stg[2] = jnp.zeros_like(tot)
        snd[0] = tot.astype(BF)
        rcopy(snd.at[0], rcv.at[0], st_send.at[1], st_recv.at[1], partners[0]).start()

    def scan_step(k):
        rcopy(snd.at[k], rcv.at[k], st_send.at[1 + k], st_recv.at[1 + k], partners[k]).wait_recv()
        got = rcv[k].astype(F32)
        upper = (q // 2 ** k) % 2
        reach = (q % 2 ** k).astype(F32)
        span = whole(2.0 * 2 ** k)
        stg[2] += jnp.where(upper == 1, whole(2.0 * reach), 0.0) * got
        if k < 4:
            tot = stg[1]
            tot = jnp.where(upper == 1, tot + span * got, span * tot + got)
            stg[1] = tot
            snd[k + 1] = tot.astype(BF)
            rcopy(snd.at[k + 1], rcv.at[k + 1], st_send.at[2 + k], st_recv.at[2 + k], partners[k + 1]).start()
        else:
            low = stg[2]
            high = whole(1.0) * low + stg[0]
            pri[c] = jnp.where(c == 0, low, high)
            stg[3] = jnp.where(c == 0, high, low)
            rcopy(stg.at[3], pri.at[c], st_send.at[6], st_recv.at[6], sib).start()

    def scan_close():
        rcopy(stg.at[3], pri.at[1 - c], st_send.at[6], st_recv.at[6], sib).wait_recv()

    def intra(h, r):
        cols = pl.ds(HD * h, HD)
        rows = pl.ds(128 * r, 128)
        seen = 128 * (r + 1)
        scores = lax.dot_general(qv[rows, cols], kv[0, :seen, cols], (((1,), (1,)), ((), ())), preferred_element_type=F32)
        probs = (scores * wts[h, rows, :seen]).astype(BF)
        att[rows, cols] = jnp.dot(probs, kv[1, :seen, cols], preferred_element_type=F32)

    def inter(h):
        cols = pl.ds(HD * h, HD)
        into = jnp.exp((pos((T, HD), 0) + 1.0) * log_decay[h])
        prior = pri[h]
        top = prior.astype(BF)
        rest = (prior - top.astype(F32)).astype(BF)
        query = qv[:, cols]
        got = jnp.dot(query, top, preferred_element_type=F32) + jnp.dot(query, rest, preferred_element_type=F32)
        full = att[:, cols] + into * got
        scale = lax.rsqrt(jnp.mean(full * full, axis=1, keepdims=True) + 1e-06)
        att[:, cols] = full * scale * gain_ref[:, HD * h:HD * (h + 1)]

    def hcopy(src_y, r, lo, n, slot, device):
        ref = hid.at[src_y, pl.ds(128 * r + lo, n), :]
        return rcopy(ref, ref, h_send.at[r, slot], h_recv.at[r, slot], device)

    def gate(r):
        rows = pl.ds(128 * r, 128)
        hid[y, rows, :] = (att[rows, :] * jax.nn.sigmoid(acc[rows, :])).astype(BF)
        hcopy(y, r, 0, 128, 0, to_yp).start()
        hcopy(y, r, 0, 128, 1, to_ym).start()

    def forward(r):
        hcopy(ym, r, 0, 128, 0, to_yp).wait_recv()
        hcopy(ym, r, 0, 64, 2, to_yp).start()
        hcopy(yp, r, 0, 128, 1, to_ym).wait_recv()
        hcopy(yp, r, 64, 64, 3, to_ym).start()

    def far(r):
        hcopy(y2, r, 0, 64, 2, to_yp).wait_recv()
        hcopy(y2, r, 64, 64, 3, to_ym).wait_recv()

    def out_part(py, first, last):
        for j in range(6):
            cols = pl.ds(F * j, F)
            w = buf[4, py, :, :, 16 * j:16 * (j + 1), :].reshape(F, F)
            part = jnp.dot(hid[py], w, preferred_element_type=F32)
            if first:
                oacc[:, cols] = part
            elif not last:
                oacc[:, cols] += part
            else:
                outv[:, cols] = (oacc[:, cols] + part).astype(BF)
                pltpu.make_async_copy(outv.at[:, cols], out_hbm.at[:, cols], out_sem.at[j]).start()

    def take(index, fn):
        def run():
            fn(index)
        return run

    def finish_k():
        kv[0] = silu(acc[...]).astype(BF)

    def finish_v():
        kv[1] = silu(acc[...]).astype(BF)

    def finish_q():
        qv[...] = silu(acc[...]).astype(BF)

    P0 = functools.partial
    tasks = []
    for item, done in ((0, finish_k), (1, finish_v)):
        for xb in range(NX):
            tasks.append((0, 0.6, P0(project, item, xb)))
        tasks.append((0, 0.3, done))
    tasks.append((0, 0.5, local_state))
    tasks.append((0, 0.2, scan_open))
    tasks.append((0, 0.6, scan_chip))
    tasks.append((0, 1.2, P0(scan_step, 0)))
    tasks.append((0, 1.2, P0(scan_step, 1)))
    tasks.append((0, 1.2, P0(scan_step, 2)))
    for xb in range(NX):
        tasks.append((1, 0.6, P0(project, 2, xb)))
    tasks.append((1, 0.3, finish_q))
    tasks.append((1, 1.2, P0(scan_step, 3)))
    for r in range(2):
        for h in range(2):
            tasks.append((1, 0.3, P0(intra, h, r)))
    tasks.append((1, 1.2, P0(scan_step, 4)))
    for r in range(2, 4):
        for h in range(2):
            tasks.append((1, 0.3, P0(intra, h, r)))
    tasks.append((1, 0.6, scan_close))
    for h in range(2):
        tasks.append((1, 0.5, P0(inter, h)))
    for xb in range(NX):
        tasks.append((2, 0.6, P0(project, 3, xb)))
    for r in range(4):
        tasks.append((2, 0.2, P0(gate, r)))
    for r in range(4):
        tasks.append((2, 1.5, P0(forward, r)))

    whole_groups = set()
    asked = set()

    def run_tasks(budget):
        while tasks and budget > 0:
            group, cost, fn = tasks[0]
            if group not in whole_groups:
                return
            if group not in asked:
                asked.add(group)
                relays_arrived(group)
                if group == 0:
                    x_load.wait()
            tasks.pop(0)
            fn()
            budget -= cost

    for slot in range(max(OFFSETS) + STAGES):
        if slot == 1:
            lax.fori_loop(0, T // 64, table, 0)
        for g in range(len(GROUPS)):
            t = slot - OFFSETS[g]
            if 0 <= t < STAGES:
                stage(g, t)
                if t == STAGES - 1:
                    whole_groups.add(g)
                run_tasks(1.2)
    run_tasks(1000.0)
    relays_arrived(3)
    out_part(y, True, False)
    out_part(ym, False, False)
    out_part(yp, False, False)
    for r in range(4):
        far(r)
    out_part(y2, False, True)

    for g in range(len(GROUPS)):
        sends_done(g)
    rcopy(state.at[1 - c], sx, st_send.at[0], st_recv.at[0], sib).wait_send()
    for k in range(5):
        rcopy(snd.at[k], rcv.at[k], st_send.at[1 + k], st_recv.at[1 + k], partners[k]).wait_send()
    rcopy(stg.at[3], pri.at[c], st_send.at[6], st_recv.at[6], sib).wait_send()
    for r in range(4):
        hcopy(y, r, 0, 128, 0, to_yp).wait_send()
        hcopy(y, r, 0, 128, 1, to_ym).wait_send()
        hcopy(ym, r, 0, 64, 2, to_yp).wait_send()
        hcopy(yp, r, 64, 64, 3, to_ym).wait_send()
    for j in range(6):
        cols = pl.ds(F * j, F)
        pltpu.make_async_copy(outv.at[:, cols], out_hbm.at[:, cols], out_sem.at[j]).wait()


def shards(inputs, proj_weight, decay_codes, norm_gain, out_weight):
    vmem = pltpu.VMEM
    dma = pltpu.SemaphoreType.DMA
    hbm = pl.BlockSpec(memory_space=pl.ANY)
    ng = len(GROUPS)
    return pl.pallas_call(
        kernel,
        out_shape=jax.ShapeDtypeStruct((T, 1536), BF),
        in_specs=[hbm, hbm, pl.BlockSpec(memory_space=pltpu.SMEM), pl.BlockSpec(memory_space=vmem), hbm],
        out_specs=hbm,
        scratch_shapes=[
            vmem((5, NX, NZ, 2, SH, F), BF),
            vmem((T, D), BF),
            vmem((2, T, T), F32),
            vmem((T, F), F32),
            vmem((2, T, F), BF),
            vmem((T, F), BF),
            vmem((T, F), F32),
            vmem((NY, T, F), BF),
            vmem((T, 1536), F32),
            vmem((T, 1536), BF),
            vmem((2, HD, HD), F32),
            vmem((HD, HD), F32),
            vmem((5, HD, HD), BF),
            vmem((5, HD, HD), BF),
            vmem((4, HD, HD), F32),
            vmem((2, HD, HD), F32),
            dma((10,)),
            dma((ng,)),
            dma((ng,)),
            dma((ng, NSLOT)),
            dma((ng, 2)),
            dma((ng, 4)),
            dma((7,)),
            dma((7,)),
            dma((4, 4)),
            dma((4, 4)),
            dma((6,)),
        ],
        compiler_params=pltpu.CompilerParams(collective_id=0, has_side_effects=True, vmem_limit_bytes=56 * 2 ** 20),
        name="lightning",
    )(inputs, proj_weight, decay_codes, norm_gain.reshape(1, F), out_weight)


def solution(mesh):
    in_specs = (P("seq", None), P(None, "seq", "tp"), P("tp"), P("tp"), P("seq", "tp"))
    out_specs = P("seq", "tp")
    return jax.shard_map(shards, mesh=mesh, in_specs=in_specs, out_specs=out_specs, check_vma=False)
```

time: 312 us -> 100 us (0.32)
  waiting for transfers between devices: 268 us -> 0 us
  Pallas kernels: 0 us -> 97.3 us
  matrix products: 21.5 us -> 0 us
  between operations: 13.2 us -> 0.01 us
  other arithmetic: 9.31 us -> 0 us
    all_gather x4 -> x0, waiting for transfers between devices: 266 us -> none  [the longest x1 96.3 us: shards(): lax.all_gather(proj_weight, 'seq', axis=1, tiled=True)]
    pallas_call x0 -> x1, Pallas kernels: none -> 97.3 us  [shards(): pl.pallas_call(kernel, out_shape=jax.ShapeDtypeStruct((T, 1536), BF), in_...]
    dot_general x5 -> x0, matrix products: 21.5 us -> none  [the longest x1 11.6 us: shards(): jnp.einsum('tr,arh->ath', columns, lax.all_gather(proj_weight, 'seq', axi...]
    dot_general x1 -> x0, other arithmetic: 4.01 us -> none  [shards(): prior = jnp.einsum('mh,mhde->hde', factor, piece, precision=high)]
  transfers between devices with their start and end apart: 4 -> 0, of which waited for: 4 -> 0; matrix products, arithmetic and copies ran while one was open for 4% -> 0% of each run, Pallas kernels for 0% -> 0%
where the time goes in v1:
time: 100 us
  Pallas kernels  97.3 us (97%)
  local copies, waits for them, and re-layouts  2.65 us (3%)
    pallas_call x1, Pallas kernels, shards(): pl.pallas_call(kernel, out_shape=jax.ShapeDtypeStruct((T, 1536), BF), in_...  97.3 us
    unnamed x1, local copies, waits for them, and re-layouts  2.65 us

profile of v1, /device:TPU:1, one launch (start us, length us, event | category | flops | bytes accessed | tf_op | source)
XLA Modules:
  0.0 100.0 jit_solution(2942349237891416769)
XLA Ops:
  0.0 97.3 %lightning.1 = bf16[512,1536]{1,0:T(8,128)(2,1)} custom-call(bf16[512,6144]{1,0:T(8,128)(2,1)} %x_hbm.1, bf16[4,96,256]{2,1,0:T(8,128)(2,1)} %wp_hbm.1, s32[2]{0:T(128)} %codes.1, f32[1,256]{1,0:T(1,128)} %bitcast.1, bf16[16,1536]{1,0:T(8,128)(2,1)} %wo_hbm.1), custom_call_target="tpu_custom_call" | custom-call | tf_op jit(solution)/shard_map/lightning/pallas_call | solution.py:452
  97.3 2.7 %copy.7 = bf16[512,1536]{1,0:T(8,128)(2,1)} copy(bf16[512,1536]{1,0:T(8,128)(2,1)} %lightning.1) | data formatting | bytes 3145728

commit v2 on v1

v2 whole, which is shorter than its diff:
```python
import functools

import jax
import jax.numpy as jnp
from jax import lax
from jax.experimental import pallas as pl
from jax.experimental.pallas import tpu as pltpu
from jax.sharding import PartitionSpec as P

NX, NZ, NY = 4, 8, 4
T = 512
D = 6144
HD = 128
F = 256
SH = 96
KX = D // NX
MESH = pl.DeviceIdType.MESH
BF = jnp.bfloat16
F32 = jnp.float32

NSLOT = 40

GROUPS = ((0, 2, 32), (2, 1, 48), (3, 1, 32), (4, 1, 32))
PLAN = (
    ("table", ((0, -1),),
     ((0, -1),)),
    ("K0", ((0, 0), (0, 1), (0, 4), (0, 5), (0, 2), (0, 12), (0, 13), (0, 20), (0, 21), (0, 6), (0, 7), (0, 28), (0, 29), (0, 14), (0, 15), (0, 22), (0, 23), (0, 8), (1, -1), (0, 9), (0, 30), (0, 31), (0, 16), (0, 17), (1, 0), (1, 1), (0, 24), (0, 25), (0, 10), (1, 2), (1, 5), (1, 4), (2, -1), (0, 11), (0, 32), (0, 33), (0, 18), (0, 19), (1, 12), (1, 13), (1, 20), (1, 21), (0, 26), (0, 27), (1, 28), (1, 29), (1, 6), (1, 7), (2, 4), (2, 5), (0, 34), (0, 35), (1, 14), (1, 15), (1, 22), (1, 23), (2, 0), (2, 1), (1, 30), (2, 2), (1, 31), (1, 8), (1, 9), (2, 6), (2, 7), (3, -1), (1, 16), (1, 17), (1, 24), (1, 25), (2, 12), (2, 13), (2, 20), (2, 21), (2, 29),),
     ((0, 0), (0, 1), (0, 8), (0, 9), (0, 12), (0, 13), (0, 2), (0, 3), (0, 16), (0, 17), (0, 10), (0, 11), (0, 14), (0, 15), (1, -1), (0, 20), (0, 21), (0, 4), (0, 5), (0, 24), (0, 25), (0, 18), (0, 19), (0, 6), (0, 7), (1, 8), (1, 9), (1, 1), (1, 0), (0, 22), (0, 23), (2, -1), (0, 28), (0, 29), (0, 32), (0, 33), (1, 3), (0, 26), (0, 27), (1, 2), (0, 36), (0, 37), (2, 0), (1, 10), (2, 1), (1, 11), (1, 16), (1, 17), (1, 12), (1, 13), (2, 8), (2, 9), (1, 5), (1, 4), (0, 30), (0, 31), (1, 7), (1, 6), (0, 34), (0, 35), (1, 24), (1, 25), (2, 2), (2, 3), (1, 20), (3, -1), (1, 21), (0, 38), (0, 39),)),
    ("K1", ((1, 32), (2, 28), (1, 33), (1, 10), (1, 11),),
     ()),
    ("K2", (),
     ((2, 12), (2, 13),)),
    ("K3", (),
     ((2, 16), (2, 17), (1, 18), (1, 19), (1, 14), (1, 15),)),
    ("finK", (),
     ((2, 10), (2, 11),)),
    ("V0", (),
     ((1, 32), (1, 33), (2, 4), (2, 5),)),
    ("V1", ((2, 8), (2, 9),),
     ((1, 28), (1, 29), (1, 36), (1, 37), (2, 6), (2, 7), (1, 26), (1, 27),)),
    ("V2", (),
     ((3, 0), (3, 1), (2, 20), (2, 21),)),
    ("V3", ((3, 4), (3, 5), (1, 18), (1, 19), (1, 26), (1, 27),),
     ((2, 24), (2, 25), (1, 22),)),
    ("finV", ((2, 14), (2, 15), (2, 22), (2, 23), (1, 34), (2, 31), (3, 1), (2, 30), (3, 0), (1, 35), (2, 10), (2, 11),),
     ((3, 9), (3, 8),)),
    ("state", (),
     ()),
    ("chip", ((3, 2), (3, 6), (3, 7),),
     ((1, 23), (2, 14), (2, 15), (3, 2), (2, 18), (2, 19), (3, 3), (1, 34), (1, 35), (2, 28), (2, 29),)),
    ("Q0", ((2, 16), (2, 17), (2, 24), (2, 25), (3, 20), (2, 33), (2, 32), (3, 21), (3, 12), (3, 13), (3, 29),),
     ((2, 32), (2, 33), (1, 30), (1, 31), (1, 38), (1, 39),)),
    ("Q1", ((3, 28),),
     ()),
    ("st0", ((3, 8), (3, 9), (2, 18), (2, 19), (2, 26),),
     ((3, 4), (2, 36), (2, 37), (3, 5), (3, 12), (3, 13), (3, 6), (3, 16), (3, 17), (3, 7), (2, 22), (2, 23),)),
    ("Q2", ((2, 27),),
     ((2, 26), (2, 27),)),
    ("Q3", ((2, 35), (3, 22), (2, 34), (3, 23), (3, 14), (3, 15),),
     ((3, 10), (3, 11),)),
    ("finQ", ((3, 31), (3, 30),),
     ((3, 20), (3, 21),)),
    ("intra0", ((3, 10), (3, 11),),
     ()),
    ("intra1", (),
     ((3, 24), (3, 25), (2, 30), (2, 31), (2, 34), (2, 35),)),
    ("st1", ((3, 24), (3, 25),),
     ((3, 28), (3, 29), (2, 38), (2, 39),)),
    ("G0", ((3, 16), (3, 17),),
     ((3, 32), (3, 33),)),
    ("G1", ((3, 33), (3, 32),),
     ((3, 14), (3, 15), (3, 18), (3, 19),)),
    ("G2", (),
     ((3, 36), (3, 37),)),
    ("G3", (),
     ((3, 22), (3, 23), (3, 26), (3, 27),)),
    ("st2", ((3, 26), (3, 27), (3, 18), (3, 19), (3, 35), (3, 34),),
     ((3, 30), (3, 31), (3, 34), (3, 35),)),
    ("inter", (),
     ((3, 38), (3, 39),)),
    ("gate0", (),
     ()),
    ("gate1", (),
     ()),
    ("gate2", (),
     ()),
    ("gate3", (),
     ()),
)


def kernel(x_hbm, wp_hbm, codes_hbm, gain_hbm, wo_hbm, out_hbm,
           codes, gain_ref, buf, xv, wts, acc, kv, qv, att, hid, oacc, outv,
           state, sx, snd, rcv, stg, pri,
           load_sem, own_send, own_recv, recv, relay_recv, send_sem,
           st_send, st_recv, h_send, h_recv, out_sem):
    s = lax.axis_index("seq")
    y = lax.axis_index("tp")
    x, z, c = s // 16, (s // 2) % 8, s % 2
    q = s // 2

    def dev(px, pz, pc, py):
        return {"seq": (px * NZ + pz) * 2 + pc, "tp": py}

    xp, xm = (x + 1) % NX, (x + 3) % NX
    zp, zm = (z + 1) % NZ, (z + 7) % NZ
    yp, ym = (y + 1) % NY, (y + 3) % NY
    x2, z4, y2 = (x + 2) % NX, (z + 4) % NZ, (y + 2) % NY
    sib = dev(x, z, 1 - c, y)
    zp2, zm2 = (z + 2) % NZ, (z + 6) % NZ
    to = {"xp": dev(xp, z, c, y), "xm": dev(xm, z, c, y), "zp": dev(x, zp, c, y), "zm": dev(x, zm, c, y),
          "x2": dev(x2, z, c, y), "zp2": dev(x, zp2, c, y), "zm2": dev(x, zm2, c, y)}
    to_y = (dev(x, z, c, yp), dev(x, z, c, ym), dev(x, z, c, y2))
    z_pair = dev(x, z + 1 - 2 * (z % 2), c, y)
    z_four = (to["zp2"], dev(x, z4, c, y), to["zm2"])
    x_four = (to["xp"], to["x2"], to["xm"])

    x_load = pltpu.make_async_copy(x_hbm, xv, load_sem.at[0])
    loads = [
        [pltpu.make_async_copy(wp_hbm.at[pl.ds(1, 2)], buf.at[pl.ds(0, 2), x, z, c], load_sem.at[1])],
        [pltpu.make_async_copy(wp_hbm.at[pl.ds(0, 1)], buf.at[pl.ds(2, 1), x, z, c], load_sem.at[2])],
        [pltpu.make_async_copy(wp_hbm.at[pl.ds(3, 1)], buf.at[pl.ds(3, 1), x, z, c], load_sem.at[3])],
        [pltpu.make_async_copy(wo_hbm.at[:, pl.ds(F * j, F)], buf.at[4, x, z, c, pl.ds(16 * j, 16), :], load_sem.at[4 + j])
         for j in range(6)],
    ]
    for group in loads:
        for copy in group:
            copy.start()
    small = [pltpu.make_async_copy(codes_hbm, codes, load_sem.at[10]),
             pltpu.make_async_copy(gain_hbm, gain_ref, load_sem.at[11])]
    for copy in small:
        copy.start()
    x_load.start()

    barrier = pltpu.get_barrier_semaphore()
    greet = list(to.values()) + [sib, z_four[1]] + list(to_y)
    for other in greet:
        pl.semaphore_signal(barrier, inc=1, device_id=other, device_id_type=MESH)
    pl.semaphore_wait(barrier, len(greet))

    def rcopy(src, dst, ssem, rsem, device):
        return pltpu.make_async_remote_copy(src, dst, ssem, rsem, device_id=device, device_id_type=MESH)

    def own_copy(g):
        i0, n, _ = GROUPS[g]
        ref = buf.at[pl.ds(i0, n), x, z, c]
        return rcopy(ref, ref, own_send.at[g], own_recv.at[g], sib)

    for g in range(len(GROUPS)):
        for copy in loads[g]:
            copy.wait()
        own_copy(g).start()

    for copy in small:
        copy.wait()
    pos = lambda shape, dim: lax.broadcasted_iota(jnp.int32, shape, dim).astype(F32)
    log_decay = [jnp.log1p(-(jnp.full((1, HD), codes[h], jnp.int32).astype(F32)) * 1e-06) for h in range(2)]
    ld_mine = jnp.where(c == 0, log_decay[0], log_decay[1])

    def table(r, carry):
        row = pos((64, T), 0) + (r * 64).astype(F32)
        diff = row - pos((64, T), 1)
        for h in range(2):
            ld = jnp.concatenate([log_decay[h]] * (T // HD), axis=1)
            w = jnp.where(diff >= 0, jnp.exp(jnp.maximum(diff, 0.0) * ld), 0.0)
            wts[h, pl.ds(pl.multiple_of(r * 64, 64), 64), :] = w
        return carry

    def piece(g, px, pz, rows, half=None):
        i0, n, _ = GROUPS[g]
        cc = pl.ds(0, 2) if half is None else pl.ds(half, 1)
        return buf.at[pl.ds(i0, n), px, pz, cc, pl.ds(*rows), :]

    def send(g, kind, ref, slot, where):
        rcopy(ref, ref, send_sem.at[g, kind], recv.at[g, slot], to[where]).start()

    def arrived(g, ref, slot):
        rcopy(ref, ref, send_sem.at[g, 0], recv.at[g, slot], sib).wait_recv()

    def relay(g, kind, ref):
        rcopy(ref, ref, send_sem.at[g, 2 + kind], relay_recv.at[g, kind], sib).start()

    def event_a(g, slot):
        pc = functools.partial(piece, g, rows=(0, GROUPS[g][2]))
        chain = lambda k, hop, way: 4 + (k * 4 + hop) * 2 + way
        columns = (x, xm, xp, x2)
        if slot < 3:
            k = slot + 1
            ref = pc(columns[k], z)
            if slot >= 0:
                arrived(g, ref, slot)
            else:
                for o, where in enumerate(("xp", "xm", "x2")):
                    send(g, 0, ref, o, where)
            send(g, 1, ref, chain(k, 0, 0), "zp")
            send(g, 1, ref, chain(k, 0, 1), "zm")
            if slot >= 0:
                relay(g, 0, ref)
            return
        k, hop, way = (slot - 4) // 8, (slot - 4) // 2 % 4, slot % 2
        pz = (z + (8 - hop - 1 if way == 0 else hop + 1)) % NZ
        ref = pc(columns[k], pz, half=way if hop == 3 else None)
        arrived(g, ref, slot)
        if hop < 3:
            part = pc(columns[k], pz, half=way if hop == 2 else None)
            send(g, 1, part, chain(k, hop + 1, way), ("zp", "zm")[way])
        relay(g, 1, ref)

    def event_b(g, slot, last):
        _, _, a = GROUPS[g]
        pc = functools.partial(piece, g, rows=(a, SH - a))
        zs = (0, -1, 1, -2, 2, -3, 3, 4)

        def across(k):
            ref = pc(x, (z + 8 + zs[k]) % NZ)
            send(g, 1, ref, 8 + 4 * k, "xp")
            send(g, 1, ref, 9 + 4 * k, "xm")

        if slot < 0:
            send(g, 0, pc(x, z), 0, "zp")
            send(g, 0, pc(x, z), 1, "zm")
            across(0)
        elif slot < 6:
            ref = pc(x, (z + 8 + zs[slot + 1]) % NZ)
            arrived(g, ref, slot)
            if slot < 4:
                send(g, 0, ref, slot + 2, ("zp", "zm")[slot % 2])
            if slot in (2, 3):
                half = pc(x, (z + 8 + zs[slot + 1]) % NZ, half=slot - 2)
                send(g, 0, half, slot + 4, ("zp2", "zm2")[slot - 2])
            across(slot + 1)
            relay(g, 0, ref)
        elif slot < 8:
            ref = pc(x, z4, half=slot - 6)
            arrived(g, ref, slot)
            relay(g, 0, ref)
            if last:
                across(7)
        else:
            k, j = (slot - 8) // 4, slot % 4
            pz = (z + 8 + zs[k]) % NZ
            ref = pc((xm, xp, x2, x2)[j], pz, half=None if j < 2 else j - 2)
            arrived(g, ref, slot)
            if j < 2:
                send(g, 1, pc((xm, xp)[j], pz, half=j), slot + 2, ("xp", "xm")[j])
            relay(g, 1, ref)

    def events(core, todo, seen):
        for g, slot in todo:
            if slot < 0:
                i0, n, _ = GROUPS[g]
                ref = buf.at[pl.ds(i0, n), x, z, 1 - c]
                rcopy(ref, ref, own_send.at[g], own_recv.at[g], sib).wait_recv()
            if core == 0:
                event_a(g, slot)
            else:
                event_b(g, slot, (g, 13 - slot) in seen)
            seen.add((g, slot))

    def sizes(g, core):
        i0, n, a = GROUPS[g]
        if core == 0:
            return [buf.at[pl.ds(i0, n), pl.ds(0, 3), 0, :, pl.ds(0, a), :],
                    buf.at[pl.ds(i0, n), :, pl.ds(0, 7), :, pl.ds(0, a), :]]
        return [buf.at[pl.ds(i0, n), 0, pl.ds(0, 7), :, pl.ds(a, SH - a), :],
                buf.at[pl.ds(i0, n), pl.ds(0, 3), :, :, pl.ds(a, SH - a), :]]

    def relays_arrived(g):
        for core in range(2):
            @pl.when(c == 1 - core)
            def _(core=core):
                for kind, ref in enumerate(sizes(g, core)):
                    rcopy(ref, ref, send_sem.at[g, 0], relay_recv.at[g, kind], sib).wait_recv()

    def sends_done(g):
        own_copy(g).wait_send()
        for core in range(2):
            @pl.when(c == core)
            def _(core=core):
                for kind, ref in enumerate(sizes(g, core)):
                    for w in (0, 2):
                        rcopy(ref, ref, send_sem.at[g, kind + w], relay_recv.at[g, 0], sib).wait_send()

    def project(item, xb):
        part = jnp.dot(xv[:, KX * xb:KX * (xb + 1)], buf[item, xb].reshape(KX, F), preferred_element_type=F32)
        if xb == 0:
            acc[...] = part
        else:
            acc[...] += part

    def silu(v):
        return v * jax.nn.sigmoid(v)

    def local_state():
        for h in range(2):
            tail = jnp.exp((T - 1.0 - pos((T, HD), 0)) * log_decay[h])
            cols = pl.ds(HD * h, HD)
            kt = (kv[0, :, cols].astype(F32) * tail).astype(BF)
            state[h] = lax.dot_general(kt, kv[1, :, cols], (((0,), (0,)), ((), ())), preferred_element_type=F32)

    whole = lambda n: jnp.exp((n * T) * ld_mine)

    def scan_open():
        rcopy(state.at[1 - c], sx, st_send.at[0, 0], st_recv.at[0, 0], sib).start()

    def scan_chip():
        rcopy(state.at[1 - c], sx, st_send.at[0, 0], st_recv.at[0, 0], sib).wait_recv()
        mine, other = state[c], sx[...]
        first = jnp.where(c == 0, mine, other)
        stg[0] = first
        stg[1] = whole(1.0) * first + jnp.where(c == 0, other, mine)
        stg[2] = jnp.zeros_like(first)

    steps = (((z_pair,), z % 2, 1, 0), (z_four, z // 2, 2, z % 2), (x_four, x, 8, z))

    def scan_send(k):
        snd[k] = stg[1].astype(BF)
        for o, other in enumerate(steps[k][0]):
            rcopy(snd.at[k], rcv.at[k, o], st_send.at[1 + k, o], st_recv.at[1 + k, o], other).start()

    def scan_step(k):
        others, place, span, reach = steps[k]
        count = len(others) + 1
        chips = lambda n: whole(2.0 * jnp.asarray(n, jnp.int32).astype(F32))
        tot = stg[1] * chips((count - 1 - place) * span)
        before = stg[2]
        for o, other in enumerate(others):
            rcopy(snd.at[k], rcv.at[k, o], st_send.at[1 + k, o], st_recv.at[1 + k, o], other).wait_recv()
            got = rcv[k, o].astype(F32)
            source = (place + count - 1 - o) % count
            before += jnp.where(place > o, chips(o * span + reach), 0.0) * got
            tot += chips((count - 1 - source) * span) * got
        stg[1] = tot
        stg[2] = before

    def scan_end():
        low = stg[2]
        high = whole(1.0) * low + stg[0]
        pri[c] = jnp.where(c == 0, low, high)
        stg[3] = jnp.where(c == 0, high, low)
        rcopy(stg.at[3], pri.at[c], st_send.at[0, 1], st_recv.at[0, 1], sib).start()

    def scan_close():
        rcopy(stg.at[3], pri.at[1 - c], st_send.at[0, 1], st_recv.at[0, 1], sib).wait_recv()

    def intra(h, r):
        cols = pl.ds(HD * h, HD)
        rows = pl.ds(128 * r, 128)
        seen = 128 * (r + 1)
        scores = lax.dot_general(qv[rows, cols], kv[0, :seen, cols], (((1,), (1,)), ((), ())), preferred_element_type=F32)
        probs = (scores * wts[h, rows, :seen]).astype(BF)
        att[rows, cols] = jnp.dot(probs, kv[1, :seen, cols], preferred_element_type=F32)

    def inter(h):
        cols = pl.ds(HD * h, HD)
        into = jnp.exp((pos((T, HD), 0) + 1.0) * log_decay[h])
        prior = pri[h]
        top = prior.astype(BF)
        rest = (prior - top.astype(F32)).astype(BF)
        query = qv[:, cols]
        got = jnp.dot(query, top, preferred_element_type=F32) + jnp.dot(query, rest, preferred_element_type=F32)
        full = att[:, cols] + into * got
        scale = lax.rsqrt(jnp.mean(full * full, axis=1, keepdims=True) + 1e-06)
        att[:, cols] = full * scale * gain_ref[:, HD * h:HD * (h + 1)]

    def hcopy(src_y, r, slot, device):
        ref = hid.at[src_y, pl.ds(128 * r, 128), :]
        return rcopy(ref, ref, h_send.at[r, slot], h_recv.at[r, slot], device)

    def gate(r):
        rows = pl.ds(128 * r, 128)
        hid[y, rows, :] = (att[rows, :] * jax.nn.sigmoid(acc[rows, :])).astype(BF)
        for o in range(3):
            hcopy(y, r, o, to_y[o]).start()

    def heads_arrived(o):
        for r in range(4):
            hcopy((ym, yp, y2)[o], r, o, to_y[o]).wait_recv()

    def out_part(py, first, last):
        for j in range(6):
            cols = pl.ds(F * j, F)
            w = buf[4, py, :, :, 16 * j:16 * (j + 1), :].reshape(F, F)
            part = jnp.dot(hid[py], w, preferred_element_type=F32)
            if first:
                oacc[:, cols] = part
            elif not last:
                oacc[:, cols] += part
            else:
                outv[:, cols] = (oacc[:, cols] + part).astype(BF)
                pltpu.make_async_copy(outv.at[:, cols], out_hbm.at[:, cols], out_sem.at[j]).start()

    def finish_k():
        kv[0] = silu(acc[...]).astype(BF)

    def finish_v():
        kv[1] = silu(acc[...]).astype(BF)

    def finish_q():
        qv[...] = silu(acc[...]).astype(BF)

    def weights(g):
        relays_arrived(g)
        if g == 0:
            x_load.wait()

    def project_all(item):
        for xb in range(NX):
            project(item, xb)

    def act(name):
        kind, n = name.rstrip("0123"), name[-1]
        n = int(n) if n.isdigit() else None
        if kind == "table":
            lax.fori_loop(0, T // 64, table, 0)
        elif kind in "KVQG":
            item = "KVQG".index(kind)
            if n == 0 and kind != "V":
                weights((0, 0, 1, 2)[item])
            project(item, n)
        elif kind == "fin" + name[-1]:
            (finish_k if n is None and name[-1] == "K" else finish_v if name[-1] == "V" else finish_q)()
        elif kind == "state":
            local_state()
            scan_open()
        elif kind == "chip":
            scan_chip()
            scan_send(0)
        elif kind == "st":
            scan_step(n)
            if n < 2:
                scan_send(n + 1)
            else:
                scan_end()
        elif kind == "intra":
            for r in range(4):
                intra(n, r)
        elif kind == "inter":
            scan_close()
            for h in range(2):
                inter(h)
        elif kind == "gate":
            gate(n)

    seen = (set(), set())
    for name, *todo in PLAN:
        for core in range(2):
            if todo[core]:
                @pl.when(c == core)
                def _(core=core, todo=todo):
                    events(core, todo[core], seen[core])
        if name:
            act(name)

    weights(3)
    out_part(y, True, False)
    heads_arrived(0)
    out_part(ym, False, False)
    heads_arrived(1)
    out_part(yp, False, False)
    heads_arrived(2)
    out_part(y2, False, True)

    for g in range(len(GROUPS)):
        sends_done(g)
    rcopy(state.at[1 - c], sx, st_send.at[0, 0], st_recv.at[0, 0], sib).wait_send()
    rcopy(stg.at[3], pri.at[c], st_send.at[0, 1], st_recv.at[0, 1], sib).wait_send()
    for k in range(3):
        for o, other in enumerate(steps[k][0]):
            rcopy(snd.at[k], rcv.at[k, o], st_send.at[1 + k, o], st_recv.at[1 + k, o], other).wait_send()
    for r in range(4):
        for o in range(3):
            hcopy(y, r, o, to_y[o]).wait_send()
    for j in range(6):
        cols = pl.ds(F * j, F)
        pltpu.make_async_copy(outv.at[:, cols], out_hbm.at[:, cols], out_sem.at[j]).wait()


def shards(inputs, proj_weight, decay_codes, norm_gain, out_weight):
    vmem = pltpu.VMEM
    dma = pltpu.SemaphoreType.DMA
    hbm = pl.BlockSpec(memory_space=pltpu.HBM)
    ng = len(GROUPS)
    args = (inputs, proj_weight, decay_codes, norm_gain.reshape(1, F), out_weight)
    args = [pltpu.with_memory_space_constraint(a, pltpu.HBM) for a in args]
    return pl.pallas_call(
        kernel,
        out_shape=jax.ShapeDtypeStruct((T, 1536), BF),
        in_specs=[hbm] * 5,
        out_specs=pl.BlockSpec(memory_space=pl.ANY),
        scratch_shapes=[
            pltpu.SMEM((2,), jnp.int32),
            vmem((1, F), F32),
            vmem((5, NX, NZ, 2, SH, F), BF),
            vmem((T, D), BF),
            vmem((2, T, T), F32),
            vmem((T, F), F32),
            vmem((2, T, F), BF),
            vmem((T, F), BF),
            vmem((T, F), F32),
            vmem((NY, T, F), BF),
            vmem((T, 1536), F32),
            vmem((T, 1536), BF),
            vmem((2, HD, HD), F32),
            vmem((HD, HD), F32),
            vmem((3, HD, HD), BF),
            vmem((3, 3, HD, HD), BF),
            vmem((4, HD, HD), F32),
            vmem((2, HD, HD), F32),
            dma((12,)),
            dma((ng,)),
            dma((ng,)),
            dma((ng, NSLOT)),
            dma((ng, 2)),
            dma((ng, 4)),
            dma((4, 3)),
            dma((4, 3)),
            dma((4, 3)),
            dma((4, 3)),
            dma((6,)),
        ],
        compiler_params=pltpu.CompilerParams(collective_id=0, has_side_effects=True, vmem_limit_bytes=52 * 2 ** 20),
        name="lightning",
    )(*args)


def solution(mesh):
    in_specs = (P("seq", None), P(None, "seq", "tp"), P("tp"), P("tp"), P("seq", "tp"))
    out_specs = P("seq", "tp")
    return jax.shard_map(shards, mesh=mesh, in_specs=in_specs, out_specs=out_specs, check_vma=False)
```

time: 100 us -> 91.2 us (0.912)
  Pallas kernels: 97.3 us -> 90 us
  local copies, waits for them, and re-layouts: 2.65 us -> 1.15 us
    pallas_call x1, Pallas kernels: 97.3 us -> 90 us  [shards(): pl.pallas_call(kernel, out_shape=jax.ShapeDtypeStruct((T, 1536), BF), in_...]
    unnamed x1, local copies, waits for them, and re-layouts: 2.65 us -> 1.15 us
where the time goes in v2:
time: 91.2 us; the launch traced here: 91.1 us
  Pallas kernels  90 us (99%)
  local copies, waits for them, and re-layouts  1.15 us (1%)
    pallas_call x1, Pallas kernels, shards(): pl.pallas_call(kernel, out_shape=jax.ShapeDtypeStruct((T, 1536), BF), in_...  90 us

profile of v2, /device:TPU:1, one launch (start us, length us, event | category | flops | bytes accessed | tf_op | source)
XLA Modules:
  0.0 91.1 jit_solution(1123366451435353605)
XLA Ops:
  0.0 90.0 %lightning.1 = bf16[512,1536]{1,0:T(8,128)(2,1)S(1)} custom-call(bf16[512,6144]{1,0:T(8,128)(2,1)} %x_hbm.1, bf16[4,96,256]{2,1,0:T(8,128)(2,1)} %wp_hbm.1, s32[2]{0:T(128)} %codes_hbm.1, f32[1,256]{1,0:T(1,128)} %bitcast.1, bf16[16,1536]{1,0:T(8,128)(2,1)} %wo_hbm.1), custom_call_target="tpu_custom_call" | custom-call | tf_op jit(solution)/shard_map/lightning/pallas_call | solution.py:486
  90.0 1.1 %copy.7 = bf16[512,1536]{1,0:T(8,128)(2,1)} copy(bf16[512,1536]{1,0:T(8,128)(2,1)S(1)} %lightning.1) | data formatting | bytes 3145728

commit v3 on v2

--- a/solution.py
+++ b/solution.py
@@ -20,64 +20,64 @@
 
 NSLOT = 40
 
-GROUPS = ((0, 2, 32), (2, 1, 48), (3, 1, 32), (4, 1, 32))
+GROUPS = ((0, 2, 32), (2, 1, 32), (3, 1, 48), (4, 1, 48))
 PLAN = (
     ("table", ((0, -1),),
      ((0, -1),)),
-    ("K0", ((0, 0), (0, 1), (0, 4), (0, 5), (0, 2), (0, 12), (0, 13), (0, 20), (0, 21), (0, 6), (0, 7), (0, 28), (0, 29), (0, 14), (0, 15), (0, 22), (0, 23), (0, 8), (1, -1), (0, 9), (0, 30), (0, 31), (0, 16), (0, 17), (1, 0), (1, 1), (0, 24), (0, 25), (0, 10), (1, 2), (1, 5), (1, 4), (2, -1), (0, 11), (0, 32), (0, 33), (0, 18), (0, 19), (1, 12), (1, 13), (1, 20), (1, 21), (0, 26), (0, 27), (1, 28), (1, 29), (1, 6), (1, 7), (2, 4), (2, 5), (0, 34), (0, 35), (1, 14), (1, 15), (1, 22), (1, 23), (2, 0), (2, 1), (1, 30), (2, 2), (1, 31), (1, 8), (1, 9), (2, 6), (2, 7), (3, -1), (1, 16), (1, 17), (1, 24), (1, 25), (2, 12), (2, 13), (2, 20), (2, 21), (2, 29),),
-     ((0, 0), (0, 1), (0, 8), (0, 9), (0, 12), (0, 13), (0, 2), (0, 3), (0, 16), (0, 17), (0, 10), (0, 11), (0, 14), (0, 15), (1, -1), (0, 20), (0, 21), (0, 4), (0, 5), (0, 24), (0, 25), (0, 18), (0, 19), (0, 6), (0, 7), (1, 8), (1, 9), (1, 1), (1, 0), (0, 22), (0, 23), (2, -1), (0, 28), (0, 29), (0, 32), (0, 33), (1, 3), (0, 26), (0, 27), (1, 2), (0, 36), (0, 37), (2, 0), (1, 10), (2, 1), (1, 11), (1, 16), (1, 17), (1, 12), (1, 13), (2, 8), (2, 9), (1, 5), (1, 4), (0, 30), (0, 31), (1, 7), (1, 6), (0, 34), (0, 35), (1, 24), (1, 25), (2, 2), (2, 3), (1, 20), (3, -1), (1, 21), (0, 38), (0, 39),)),
-    ("K1", ((1, 32), (2, 28), (1, 33), (1, 10), (1, 11),),
-     ()),
-    ("K2", (),
-     ((2, 12), (2, 13),)),
-    ("K3", (),
-     ((2, 16), (2, 17), (1, 18), (1, 19), (1, 14), (1, 15),)),
-    ("finK", (),
-     ((2, 10), (2, 11),)),
+    ("K0", ((0, 0), (0, 1), (0, 4), (0, 5), (0, 2), (0, 12), (0, 13), (0, 20), (0, 21), (0, 6), (0, 7), (0, 28), (0, 29), (1, -1), (0, 14), (0, 15), (0, 22), (0, 23), (0, 8), (0, 9), (0, 30), (0, 31), (1, 4), (1, 5), (1, 0), (1, 1), (1, 2), (0, 16), (0, 17), (2, -1), (0, 24), (0, 25), (0, 10), (0, 11),),
+     ((0, 0), (0, 1), (0, 8), (0, 9), (0, 12), (0, 13), (0, 2), (0, 3), (0, 16), (0, 17), (1, -1), (0, 10), (0, 11), (0, 14), (0, 15), (0, 20), (0, 21), (0, 4), (0, 5), (0, 24), (0, 25), (0, 18), (0, 19), (0, 6), (0, 7), (1, 0), (1, 1), (1, 8), (1, 9), (2, -1), (0, 22), (0, 23), (0, 28), (0, 29),)),
     ("V0", (),
-     ((1, 32), (1, 33), (2, 4), (2, 5),)),
-    ("V1", ((2, 8), (2, 9),),
-     ((1, 28), (1, 29), (1, 36), (1, 37), (2, 6), (2, 7), (1, 26), (1, 27),)),
-    ("V2", (),
-     ((3, 0), (3, 1), (2, 20), (2, 21),)),
-    ("V3", ((3, 4), (3, 5), (1, 18), (1, 19), (1, 26), (1, 27),),
-     ((2, 24), (2, 25), (1, 22),)),
-    ("finV", ((2, 14), (2, 15), (2, 22), (2, 23), (1, 34), (2, 31), (3, 1), (2, 30), (3, 0), (1, 35), (2, 10), (2, 11),),
-     ((3, 9), (3, 8),)),
+     ()),
+    ("K1", ((0, 32), (0, 33), (1, 6), (1, 7), (1, 12), (1, 13), (1, 20), (1, 21), (1, 28), (1, 29), (0, 18), (0, 19), (2, 4), (2, 5), (0, 26), (0, 27), (0, 34), (0, 35), (1, 8), (1, 9), (1, 14), (1, 15),),
+     ((0, 32), (0, 33), (1, 2), (1, 3), (0, 26), (0, 27), (2, 1), (2, 0), (0, 36), (0, 37), (1, 12), (1, 13),)),
+    ("K2", ((3, -1), (1, 22), (1, 23),),
+     ((1, 16), (1, 17),)),
+    ("V1", ((2, 0), (2, 1),),
+     ((3, -1), (1, 10), (1, 11), (2, 8), (2, 9), (1, 4), (1, 5),)),
+    ("V2", ((1, 30), (1, 31),),
+     ()),
+    ("Q0", ((2, 2), (2, 6), (2, 7), (1, 10), (1, 11), (1, 16), (1, 17),),
+     ((1, 6), (1, 7), (2, 2), (2, 3), (0, 30), (0, 31), (0, 34), (0, 35), (1, 20), (1, 21),)),
+    ("K3", ((3, 4), (3, 5), (1, 24), (1, 25), (2, 12), (2, 13), (2, 20), (2, 21), (1, 32), (1, 33), (2, 29), (3, 0), (3, 1), (2, 28),),
+     ((3, 0), (3, 1), (1, 24), (1, 25), (2, 16), (2, 17), (2, 12), (2, 13), (0, 38), (0, 39),)),
+    ("V3", ((2, 8), (2, 9), (1, 18), (1, 19), (3, 2),),
+     ((1, 14), (1, 15), (2, 4), (1, 18), (1, 19), (2, 5),)),
+    ("finK", ((3, 6), (3, 7), (1, 26), (1, 27),),
+     ((2, 6),)),
+    ("finV", (),
+     ()),
     ("state", (),
      ()),
-    ("chip", ((3, 2), (3, 6), (3, 7),),
-     ((1, 23), (2, 14), (2, 15), (3, 2), (2, 18), (2, 19), (3, 3), (1, 34), (1, 35), (2, 28), (2, 29),)),
-    ("Q0", ((2, 16), (2, 17), (2, 24), (2, 25), (3, 20), (2, 33), (2, 32), (3, 21), (3, 12), (3, 13), (3, 29),),
-     ((2, 32), (2, 33), (1, 30), (1, 31), (1, 38), (1, 39),)),
-    ("Q1", ((3, 28),),
-     ()),
-    ("st0", ((3, 8), (3, 9), (2, 18), (2, 19), (2, 26),),
-     ((3, 4), (2, 36), (2, 37), (3, 5), (3, 12), (3, 13), (3, 6), (3, 16), (3, 17), (3, 7), (2, 22), (2, 23),)),
-    ("Q2", ((2, 27),),
-     ((2, 26), (2, 27),)),
-    ("Q3", ((2, 35), (3, 22), (2, 34), (3, 23), (3, 14), (3, 15),),
-     ((3, 10), (3, 11),)),
-    ("finQ", ((3, 31), (3, 30),),
-     ((3, 20), (3, 21),)),
-    ("intra0", ((3, 10), (3, 11),),
-     ()),
-    ("intra1", (),
-     ((3, 24), (3, 25), (2, 30), (2, 31), (2, 34), (2, 35),)),
-    ("st1", ((3, 24), (3, 25),),
-     ((3, 28), (3, 29), (2, 38), (2, 39),)),
-    ("G0", ((3, 16), (3, 17),),
-     ((3, 32), (3, 33),)),
-    ("G1", ((3, 33), (3, 32),),
-     ((3, 14), (3, 15), (3, 18), (3, 19),)),
+    ("chip", ((2, 14), (2, 15),),
+     ((2, 7), (3, 8), (3, 9), (2, 10), (2, 11), (1, 28), (1, 29), (3, 2), (3, 3), (1, 32), (1, 33), (1, 36), (1, 37), (2, 20), (2, 21),)),
+    ("Q1", ((2, 22), (2, 23), (1, 34), (1, 35), (3, 12), (2, 31), (3, 20), (3, 13),),
+     ()),
+    ("Q2", ((2, 30), (3, 21), (2, 10), (2, 11),),
+     ((2, 24), (2, 25), (1, 22), (1, 23),)),
+    ("G0", ((3, 28), (3, 29),),
+     ((3, 12), (3, 13), (3, 16), (3, 17), (1, 26), (1, 27), (2, 18), (2, 19), (2, 14), (2, 15), (3, 4), (3, 5),)),
+    ("st0", ((3, 8), (3, 9), (2, 16), (2, 17),),
+     ((2, 28), (2, 29), (2, 32), (2, 33), (3, 6), (3, 7), (2, 36), (2, 37), (3, 10), (3, 11), (1, 30), (1, 31),)),
+    ("G1", ((2, 24), (2, 25), (3, 14), (2, 33), (3, 22), (3, 15), (2, 32), (3, 23), (3, 30), (3, 31), (3, 10), (3, 11), (2, 18), (2, 19),),
+     ((3, 20), (3, 21), (3, 24), (3, 25), (1, 34), (1, 35), (1, 38), (1, 39), (2, 22), (2, 23), (2, 26), (2, 27), (3, 14), (3, 15), (3, 18), (3, 19), (3, 28), (3, 29),)),
+    ("Q3", (),
+     ((3, 32), (3, 33), (2, 30), (2, 31), (2, 34), (2, 35),)),
+    ("finQ", (),
+     ((3, 36), (3, 37), (2, 38), (2, 39), (3, 22), (3, 23), (3, 26), (3, 27),)),
+    ("intra0", (),
+     ((3, 30), (3, 31),)),
+    ("intra1", ((2, 26), (2, 27),),
+     ((3, 34),)),
+    ("st1", ((2, 35), (3, 16),),
+     ((3, 35),)),
     ("G2", (),
-     ((3, 36), (3, 37),)),
-    ("G3", (),
-     ((3, 22), (3, 23), (3, 26), (3, 27),)),
-    ("st2", ((3, 26), (3, 27), (3, 18), (3, 19), (3, 35), (3, 34),),
-     ((3, 30), (3, 31), (3, 34), (3, 35),)),
-    ("inter", (),
+     ()),
+    ("G3", ((3, 17), (3, 24), (2, 34), (3, 25),),
+     ()),
+    ("st2", ((3, 32), (3, 33), (3, 18),),
      ((3, 38), (3, 39),)),
+    ("inter", ((3, 19), (3, 26), (3, 27), (3, 34), (3, 35),),
+     ()),
     ("gate0", (),
      ()),
     ("gate1", (),
@@ -85,6 +85,22 @@
     ("gate2", (),
      ()),
     ("gate3", (),
+     ()),
+    ("out0", (),
+     ()),
+    ("fwd0", (),
+     ()),
+    ("fwd1", (),
+     ()),
+    ("fwd2", (),
+     ()),
+    ("fwd3", (),
+     ()),
+    ("out1", (),
+     ()),
+    ("out2", (),
+     ()),
+    ("out3", (),
      ()),
 )
 
@@ -92,7 +108,7 @@
 def kernel(x_hbm, wp_hbm, codes_hbm, gain_hbm, wo_hbm, out_hbm,
            codes, gain_ref, buf, xv, wts, acc, kv, qv, att, hid, oacc, outv,
            state, sx, snd, rcv, stg, pri,
-           load_sem, own_send, own_recv, recv, relay_recv, send_sem,
+           load_sem, own_send, own_recv, recv, relay_recv, relay_send, send_sem,
            st_send, st_recv, h_send, h_recv, out_sem):
     s = lax.axis_index("seq")
     y = lax.axis_index("tp")
@@ -110,7 +126,7 @@
     zp2, zm2 = (z + 2) % NZ, (z + 6) % NZ
     to = {"xp": dev(xp, z, c, y), "xm": dev(xm, z, c, y), "zp": dev(x, zp, c, y), "zm": dev(x, zm, c, y),
           "x2": dev(x2, z, c, y), "zp2": dev(x, zp2, c, y), "zm2": dev(x, zm2, c, y)}
-    to_y = (dev(x, z, c, yp), dev(x, z, c, ym), dev(x, z, c, y2))
+    to_y = (dev(x, z, c, yp), dev(x, z, c, ym))
     z_pair = dev(x, z + 1 - 2 * (z % 2), c, y)
     z_four = (to["zp2"], dev(x, z4, c, y), to["zm2"])
     x_four = (to["xp"], to["x2"], to["xm"])
@@ -177,8 +193,8 @@
     def arrived(g, ref, slot):
         rcopy(ref, ref, send_sem.at[g, 0], recv.at[g, slot], sib).wait_recv()
 
-    def relay(g, kind, ref):
-        rcopy(ref, ref, send_sem.at[g, 2 + kind], relay_recv.at[g, kind], sib).start()
+    def relay(g, column, ref):
+        rcopy(ref, ref, relay_send.at[g, column], relay_recv.at[g, column], sib).start()
 
     def event_a(g, slot):
         pc = functools.partial(piece, g, rows=(0, GROUPS[g][2]))
@@ -195,7 +211,7 @@
             send(g, 1, ref, chain(k, 0, 0), "zp")
             send(g, 1, ref, chain(k, 0, 1), "zm")
             if slot >= 0:
-                relay(g, 0, ref)
+                relay(g, k, ref)
             return
         k, hop, way = (slot - 4) // 8, (slot - 4) // 2 % 4, slot % 2
         pz = (z + (8 - hop - 1 if way == 0 else hop + 1)) % NZ
@@ -204,7 +220,7 @@
         if hop < 3:
             part = pc(columns[k], pz, half=way if hop == 2 else None)
             send(g, 1, part, chain(k, hop + 1, way), ("zp", "zm")[way])
-        relay(g, 1, ref)
+        relay(g, k, ref)
 
     def event_b(g, slot, last):
         _, _, a = GROUPS[g]
@@ -243,7 +259,7 @@
             arrived(g, ref, slot)
             if j < 2:
                 send(g, 1, pc((xm, xp)[j], pz, half=j), slot + 2, ("xp", "xm")[j])
-            relay(g, 1, ref)
+            relay(g, (1, 2, 3, 3)[j], ref)
 
     def events(core, todo, seen):
         for g, slot in todo:
@@ -265,12 +281,17 @@
         return [buf.at[pl.ds(i0, n), 0, pl.ds(0, 7), :, pl.ds(a, SH - a), :],
                 buf.at[pl.ds(i0, n), pl.ds(0, 3), :, :, pl.ds(a, SH - a), :]]
 
-    def relays_arrived(g):
+    def column_size(g, core, column):
+        i0, n, a = GROUPS[g]
+        rows = pl.ds(0, a) if core == 0 else pl.ds(a, SH - a)
+        return buf.at[pl.ds(i0, n), 0, pl.ds(0, 7 if column == 0 else 8), :, rows, :]
+
+    def relays_arrived(g, column):
         for core in range(2):
             @pl.when(c == 1 - core)
             def _(core=core):
-                for kind, ref in enumerate(sizes(g, core)):
-                    rcopy(ref, ref, send_sem.at[g, 0], relay_recv.at[g, kind], sib).wait_recv()
+                ref = column_size(g, core, column)
+                rcopy(ref, ref, relay_send.at[g, 0], relay_recv.at[g, column], sib).wait_recv()
 
     def sends_done(g):
         own_copy(g).wait_send()
@@ -278,15 +299,19 @@
             @pl.when(c == core)
             def _(core=core):
                 for kind, ref in enumerate(sizes(g, core)):
-                    for w in (0, 2):
-                        rcopy(ref, ref, send_sem.at[g, kind + w], relay_recv.at[g, 0], sib).wait_send()
-
-    def project(item, xb):
-        part = jnp.dot(xv[:, KX * xb:KX * (xb + 1)], buf[item, xb].reshape(KX, F), preferred_element_type=F32)
-        if xb == 0:
-            acc[...] = part
+                    rcopy(ref, ref, send_sem.at[g, kind], recv.at[g, 0], sib).wait_send()
+                for column in range(NX):
+                    ref = column_size(g, core, column)
+                    rcopy(ref, ref, relay_send.at[g, column], relay_recv.at[g, 0], sib).wait_send()
+
+    def project(item, k):
+        px = (x, xm, xp, x2)[k]
+        cols = pl.ds(pl.multiple_of(px * KX, KX), KX)
+        part = jnp.dot(xv[:, cols], buf[item, px].reshape(KX, F), preferred_element_type=F32)
+        if k == 0:
+            acc[item] = part
         else:
-            acc[...] += part
+            acc[item] += part
 
     def silu(v):
         return v * jax.nn.sigmoid(v)
@@ -363,19 +388,25 @@
         scale = lax.rsqrt(jnp.mean(full * full, axis=1, keepdims=True) + 1e-06)
         att[:, cols] = full * scale * gain_ref[:, HD * h:HD * (h + 1)]
 
-    def hcopy(src_y, r, slot, device):
-        ref = hid.at[src_y, pl.ds(128 * r, 128), :]
-        return rcopy(ref, ref, h_send.at[r, slot], h_recv.at[r, slot], device)
+    def hcopy(src_y, r, lo, n, slot):
+        ref = hid.at[src_y, pl.ds(128 * r + lo, n), :]
+        return rcopy(ref, ref, h_send.at[r, slot], h_recv.at[r, slot], to_y[slot % 2])
 
     def gate(r):
         rows = pl.ds(128 * r, 128)
-        hid[y, rows, :] = (att[rows, :] * jax.nn.sigmoid(acc[rows, :])).astype(BF)
-        for o in range(3):
-            hcopy(y, r, o, to_y[o]).start()
-
-    def heads_arrived(o):
-        for r in range(4):
-            hcopy((ym, yp, y2)[o], r, o, to_y[o]).wait_recv()
+        hid[y, rows, :] = (att[rows, :] * jax.nn.sigmoid(acc[3, rows, :])).astype(BF)
+        hcopy(y, r, 0, 128, 0).start()
+        hcopy(y, r, 0, 128, 1).start()
+
+    def forward(r):
+        hcopy(ym, r, 0, 128, 0).wait_recv()
+        hcopy(ym, r, 0, 64, 2).start()
+        hcopy(yp, r, 0, 128, 1).wait_recv()
+        hcopy(yp, r, 64, 64, 3).start()
+
+    def far(r):
+        hcopy(y2, r, 0, 64, 2).wait_recv()
+        hcopy(y2, r, 64, 64, 3).wait_recv()
 
     def out_part(py, first, last):
         for j in range(6):
@@ -391,22 +422,18 @@
                 pltpu.make_async_copy(outv.at[:, cols], out_hbm.at[:, cols], out_sem.at[j]).start()
 
     def finish_k():
-        kv[0] = silu(acc[...]).astype(BF)
+        kv[0] = silu(acc[0]).astype(BF)
 
     def finish_v():
-        kv[1] = silu(acc[...]).astype(BF)
+        kv[1] = silu(acc[1]).astype(BF)
 
     def finish_q():
-        qv[...] = silu(acc[...]).astype(BF)
-
-    def weights(g):
-        relays_arrived(g)
-        if g == 0:
+        qv[...] = silu(acc[2]).astype(BF)
+
+    def weights(g, k):
+        relays_arrived(g, k)
+        if (g, k) == (0, 0):
             x_load.wait()
-
-    def project_all(item):
-        for xb in range(NX):
-            project(item, xb)
 
     def act(name):
         kind, n = name.rstrip("0123"), name[-1]
@@ -415,8 +442,8 @@
             lax.fori_loop(0, T // 64, table, 0)
         elif kind in "KVQG":
             item = "KVQG".index(kind)
-            if n == 0 and kind != "V":
-                weights((0, 0, 1, 2)[item])
+            if kind != "V":
+                weights((0, 0, 1, 2)[item], n)
             project(item, n)
         elif kind == "fin" + name[-1]:
             (finish_k if n is None and name[-1] == "K" else finish_v if name[-1] == "V" else finish_q)()
@@ -441,6 +468,16 @@
                 inter(h)
         elif kind == "gate":
             gate(n)
+        elif kind == "fwd":
+            forward(n)
+        elif kind == "out":
+            if n == 0:
+                for k in range(NX):
+                    weights(3, k)
+            if n == 3:
+                for r in range(4):
+                    far(r)
+            out_part((y, ym, yp, y2)[n], n == 0, n == 3)
 
     seen = (set(), set())
     for name, *todo in PLAN:
@@ -452,15 +489,6 @@
         if name:
             act(name)
 
-    weights(3)
-    out_part(y, True, False)
-    heads_arrived(0)
-    out_part(ym, False, False)
-    heads_arrived(1)
-    out_part(yp, False, False)
-    heads_arrived(2)
-    out_part(y2, False, True)
-
     for g in range(len(GROUPS)):
         sends_done(g)
     rcopy(state.at[1 - c], sx, st_send.at[0, 0], st_recv.at[0, 0], sib).wait_send()
@@ -469,8 +497,10 @@
         for o, other in enumerate(steps[k][0]):
             rcopy(snd.at[k], rcv.at[k, o], st_send.at[1 + k, o], st_recv.at[1 + k, o], other).wait_send()
     for r in range(4):
-        for o in range(3):
-            hcopy(y, r, o, to_y[o]).wait_send()
+        hcopy(y, r, 0, 128, 0).wait_send()
+        hcopy(y, r, 0, 128, 1).wait_send()
+        hcopy(ym, r, 0, 64, 2).wait_send()
+        hcopy(yp, r, 64, 64, 3).wait_send()
     for j in range(6):
         cols = pl.ds(F * j, F)
         pltpu.make_async_copy(outv.at[:, cols], out_hbm.at[:, cols], out_sem.at[j]).wait()
@@ -494,7 +524,7 @@
             vmem((5, NX, NZ, 2, SH, F), BF),
             vmem((T, D), BF),
             vmem((2, T, T), F32),
-            vmem((T, F), F32),
+            vmem((4, T, F), F32),
             vmem((2, T, F), BF),
             vmem((T, F), BF),
             vmem((T, F), F32),
@@ -511,12 +541,13 @@
             dma((ng,)),
             dma((ng,)),
             dma((ng, NSLOT)),
+            dma((ng, NX)),
+            dma((ng, NX)),
             dma((ng, 2)),
-            dma((ng, 4)),
             dma((4, 3)),
             dma((4, 3)),
-            dma((4, 3)),
-            dma((4, 3)),
+            dma((4, 4)),
+            dma((4, 4)),
             dma((6,)),
         ],
         compiler_params=pltpu.CompilerParams(collective_id=0, has_side_effects=True, vmem_limit_bytes=52 * 2 ** 20),

time: 91.2 us -> 83 us (0.910)
  Pallas kernels: 90 us -> 81.1 us
    pallas_call x1, Pallas kernels: 90 us -> 81.1 us  [shards(): pl.pallas_call(kernel, out_shape=jax.ShapeDtypeStruct((T, 1536), BF), in_...]
where the time goes in v3:
time: 83 us; the launch traced here: 82.2 us
  Pallas kernels  81.1 us (98%)
  local copies, waits for them, and re-layouts  1.15 us (1%)
    pallas_call x1, Pallas kernels, shards(): pl.pallas_call(kernel, out_shape=jax.ShapeDtypeStruct((T, 1536), BF), in_...  81.1 us

profile of v3, /device:TPU:1, one launch (start us, length us, event | category | flops | bytes accessed | tf_op | source)
XLA Modules:
  0.0 82.2 jit_solution(2256333517900568062)
XLA Ops:
  0.0 81.1 %lightning.1 = bf16[512,1536]{1,0:T(8,128)(2,1)S(1)} custom-call(bf16[512,6144]{1,0:T(8,128)(2,1)} %x_hbm.1, bf16[4,96,256]{2,1,0:T(8,128)(2,1)} %wp_hbm.1, s32[2]{0:T(128)} %codes_hbm.1, f32[1,256]{1,0:T(1,128)} %bitcast.1, bf16[16,1536]{1,0:T(8,128)(2,1)} %wo_hbm.1), custom_call_target="tpu_custom_call" | custom-call | tf_op jit(solution)/shard_map/lightning/pallas_call | solution.py:516
  81.1 1.1 %copy.7 = bf16[512,1536]{1,0:T(8,128)(2,1)} copy(bf16[512,1536]{1,0:T(8,128)(2,1)S(1)} %lightning.1) | data formatting | bytes 3145728

commit v4 on v3

--- a/solution.py
+++ b/solution.py
@@ -20,64 +20,64 @@
 
 NSLOT = 40
 
-GROUPS = ((0, 2, 32), (2, 1, 32), (3, 1, 48), (4, 1, 48))
+GROUPS = ((0, 2, 32), (2, 1, 32), (3, 1, 48), (4, 1, 32))
 PLAN = (
     ("table", ((0, -1),),
      ((0, -1),)),
-    ("K0", ((0, 0), (0, 1), (0, 4), (0, 5), (0, 2), (0, 12), (0, 13), (0, 20), (0, 21), (0, 6), (0, 7), (0, 28), (0, 29), (1, -1), (0, 14), (0, 15), (0, 22), (0, 23), (0, 8), (0, 9), (0, 30), (0, 31), (1, 4), (1, 5), (1, 0), (1, 1), (1, 2), (0, 16), (0, 17), (2, -1), (0, 24), (0, 25), (0, 10), (0, 11),),
-     ((0, 0), (0, 1), (0, 8), (0, 9), (0, 12), (0, 13), (0, 2), (0, 3), (0, 16), (0, 17), (1, -1), (0, 10), (0, 11), (0, 14), (0, 15), (0, 20), (0, 21), (0, 4), (0, 5), (0, 24), (0, 25), (0, 18), (0, 19), (0, 6), (0, 7), (1, 0), (1, 1), (1, 8), (1, 9), (2, -1), (0, 22), (0, 23), (0, 28), (0, 29),)),
-    ("V0", (),
-     ()),
-    ("K1", ((0, 32), (0, 33), (1, 6), (1, 7), (1, 12), (1, 13), (1, 20), (1, 21), (1, 28), (1, 29), (0, 18), (0, 19), (2, 4), (2, 5), (0, 26), (0, 27), (0, 34), (0, 35), (1, 8), (1, 9), (1, 14), (1, 15),),
-     ((0, 32), (0, 33), (1, 2), (1, 3), (0, 26), (0, 27), (2, 1), (2, 0), (0, 36), (0, 37), (1, 12), (1, 13),)),
-    ("K2", ((3, -1), (1, 22), (1, 23),),
-     ((1, 16), (1, 17),)),
-    ("V1", ((2, 0), (2, 1),),
-     ((3, -1), (1, 10), (1, 11), (2, 8), (2, 9), (1, 4), (1, 5),)),
-    ("V2", ((1, 30), (1, 31),),
-     ()),
-    ("Q0", ((2, 2), (2, 6), (2, 7), (1, 10), (1, 11), (1, 16), (1, 17),),
-     ((1, 6), (1, 7), (2, 2), (2, 3), (0, 30), (0, 31), (0, 34), (0, 35), (1, 20), (1, 21),)),
-    ("K3", ((3, 4), (3, 5), (1, 24), (1, 25), (2, 12), (2, 13), (2, 20), (2, 21), (1, 32), (1, 33), (2, 29), (3, 0), (3, 1), (2, 28),),
-     ((3, 0), (3, 1), (1, 24), (1, 25), (2, 16), (2, 17), (2, 12), (2, 13), (0, 38), (0, 39),)),
-    ("V3", ((2, 8), (2, 9), (1, 18), (1, 19), (3, 2),),
-     ((1, 14), (1, 15), (2, 4), (1, 18), (1, 19), (2, 5),)),
-    ("finK", ((3, 6), (3, 7), (1, 26), (1, 27),),
-     ((2, 6),)),
+    ("K0", ((0, 0), (0, 1), (0, 4), (0, 5), (0, 2), (0, 12), (0, 13), (0, 20), (0, 21), (0, 6), (0, 7), (1, -1), (0, 28), (0, 29), (0, 14), (0, 15), (1, 0), (1, 1), (0, 22), (0, 23), (1, 2), (0, 8), (0, 9), (1, 4), (1, 5), (0, 30), (0, 31), (2, -1), (0, 16), (0, 17), (1, 12), (1, 13), (1, 20), (1, 21), (0, 24), (0, 25), (1, 28), (1, 29), (2, 0), (2, 1), (0, 10), (0, 11),),
+     ((0, 0), (0, 1), (0, 8), (0, 9), (1, -1), (0, 12), (0, 13), (0, 2), (0, 3), (0, 16), (0, 17), (0, 10), (0, 11), (1, 8), (1, 9), (0, 14), (0, 15), (1, 0), (1, 1), (2, -1), (0, 20), (0, 21), (0, 4), (0, 5), (0, 24), (0, 25), (0, 18), (0, 19), (1, 10), (1, 11), (0, 6), (0, 7), (1, 12), (1, 13), (1, 16), (1, 17), (2, 8), (2, 9), (0, 22), (0, 23), (1, 2), (1, 3),)),
+    ("V0", ((1, 6), (1, 7), (2, 2),),
+     ()),
+    ("K1", ((0, 32), (0, 33), (2, 4), (2, 5), (0, 18), (0, 19), (1, 14), (1, 15), (1, 22), (1, 23), (0, 26), (0, 27), (1, 30), (1, 31), (2, 12), (2, 13), (2, 20), (2, 21), (1, 8), (1, 9), (2, 28), (2, 29),),
+     ((2, 0), (2, 1), (0, 28), (0, 29), (0, 32), (0, 33), (0, 26), (0, 27), (0, 36), (0, 37),)),
+    ("K2", (),
+     ((1, 14), (1, 15), (1, 18), (1, 19), (2, 10), (2, 11),)),
+    ("V1", ((0, 34), (0, 35),),
+     ((1, 4), (1, 5), (1, 20), (1, 21),)),
+    ("V2", ((3, -1),),
+     ((1, 24), (1, 25), (1, 6), (3, -1), (1, 7), (2, 2), (2, 3), (2, 12), (2, 13), (2, 16), (2, 17),)),
+    ("Q0", ((2, 6), (2, 7), (1, 16), (1, 17), (1, 24), (1, 25), (1, 32), (1, 33), (2, 14), (2, 15), (2, 22), (2, 23), (1, 10), (1, 11),),
+     ((0, 30), (0, 31), (0, 34), (0, 35), (0, 38), (0, 39), (1, 28), (1, 29), (3, 0), (3, 1), (1, 32), (1, 33), (1, 22), (1, 23),)),
+    ("K3", ((2, 30), (2, 31),),
+     ((1, 26), (1, 27), (2, 4), (2, 5), (3, 8), (3, 9),)),
+    ("V3", ((3, 4), (3, 5),),
+     ((2, 6), (2, 7), (1, 36), (1, 37),)),
+    ("finK", (),
+     ()),
     ("finV", (),
      ()),
     ("state", (),
      ()),
-    ("chip", ((2, 14), (2, 15),),
-     ((2, 7), (3, 8), (3, 9), (2, 10), (2, 11), (1, 28), (1, 29), (3, 2), (3, 3), (1, 32), (1, 33), (1, 36), (1, 37), (2, 20), (2, 21),)),
-    ("Q1", ((2, 22), (2, 23), (1, 34), (1, 35), (3, 12), (2, 31), (3, 20), (3, 13),),
-     ()),
-    ("Q2", ((2, 30), (3, 21), (2, 10), (2, 11),),
-     ((2, 24), (2, 25), (1, 22), (1, 23),)),
-    ("G0", ((3, 28), (3, 29),),
-     ((3, 12), (3, 13), (3, 16), (3, 17), (1, 26), (1, 27), (2, 18), (2, 19), (2, 14), (2, 15), (3, 4), (3, 5),)),
-    ("st0", ((3, 8), (3, 9), (2, 16), (2, 17),),
-     ((2, 28), (2, 29), (2, 32), (2, 33), (3, 6), (3, 7), (2, 36), (2, 37), (3, 10), (3, 11), (1, 30), (1, 31),)),
-    ("G1", ((2, 24), (2, 25), (3, 14), (2, 33), (3, 22), (3, 15), (2, 32), (3, 23), (3, 30), (3, 31), (3, 10), (3, 11), (2, 18), (2, 19),),
-     ((3, 20), (3, 21), (3, 24), (3, 25), (1, 34), (1, 35), (1, 38), (1, 39), (2, 22), (2, 23), (2, 26), (2, 27), (3, 14), (3, 15), (3, 18), (3, 19), (3, 28), (3, 29),)),
+    ("chip", ((2, 8), (2, 9), (1, 18), (1, 19), (1, 26), (1, 27), (1, 34), (1, 35), (3, 0), (3, 1), (2, 16), (2, 17), (3, 2), (2, 24), (2, 25), (2, 32), (2, 33),),
+     ((2, 20), (2, 21), (2, 24), (2, 25),)),
+    ("Q1", ((3, 6), (3, 7),),
+     ((2, 14), (2, 15), (2, 18), (2, 19),)),
+    ("Q2", ((2, 10), (2, 11), (3, 12), (3, 13), (3, 20), (3, 21), (2, 18), (2, 19),),
+     ((3, 2), (3, 3), (1, 30), (1, 31), (3, 12), (3, 13),)),
+    ("G0", ((3, 28), (3, 29), (2, 26), (2, 27), (2, 34), (2, 35),),
+     ((3, 16), (3, 17), (1, 34), (1, 35), (2, 28), (2, 29),)),
+    ("st0", (),
+     ((2, 32), (2, 33),)),
+    ("G1", ((3, 8), (3, 9), (3, 14), (3, 15),),
+     ((3, 10), (3, 11), (3, 4), (3, 5), (2, 36), (2, 37),)),
+    ("G2", ((3, 22), (3, 23), (3, 30), (3, 31),),
+     ((1, 38), (1, 39), (2, 22), (2, 23), (2, 26), (2, 27), (3, 6), (3, 7),)),
     ("Q3", (),
-     ((3, 32), (3, 33), (2, 30), (2, 31), (2, 34), (2, 35),)),
+     ((3, 20), (3, 21),)),
     ("finQ", (),
-     ((3, 36), (3, 37), (2, 38), (2, 39), (3, 22), (3, 23), (3, 26), (3, 27),)),
+     ((3, 24), (3, 25), (3, 14), (3, 15),)),
     ("intra0", (),
-     ((3, 30), (3, 31),)),
-    ("intra1", ((2, 26), (2, 27),),
-     ((3, 34),)),
-    ("st1", ((2, 35), (3, 16),),
-     ((3, 35),)),
-    ("G2", (),
-     ()),
-    ("G3", ((3, 17), (3, 24), (2, 34), (3, 25),),
-     ()),
-    ("st2", ((3, 32), (3, 33), (3, 18),),
-     ((3, 38), (3, 39),)),
-    ("inter", ((3, 19), (3, 26), (3, 27), (3, 34), (3, 35),),
-     ()),
+     ((3, 18), (3, 19),)),
+    ("st1", ((3, 10), (3, 11),),
+     ((2, 30), (2, 31), (2, 34), (2, 35),)),
+    ("intra1", ((3, 16), (3, 17), (3, 24), (3, 25),),
+     ()),
+    ("G3", ((3, 32), (3, 33),),
+     ((3, 28), (3, 29), (3, 32), (3, 33), (2, 38), (2, 39),)),
+    ("st2", ((3, 18), (3, 19), (3, 26), (3, 27), (3, 34), (3, 35),),
+     ((3, 36), (3, 37), (3, 22), (3, 23), (3, 26), (3, 27), (3, 30), (3, 31),)),
+    ("inter", (),
+     ((3, 34), (3, 35), (3, 38), (3, 39),)),
     ("gate0", (),
      ()),
     ("gate1", (),
@@ -105,11 +105,11 @@
 )
 
 
-def kernel(x_hbm, wp_hbm, codes_hbm, gain_hbm, wo_hbm, out_hbm,
-           codes, gain_ref, buf, xv, wts, acc, kv, qv, att, hid, oacc, outv,
+def kernel(x_hbm, wp_hbm, codes_hbm, gain_hbm, wo_hbm, out_ref,
+           codes, gain_ref, buf, xv, wts, acc, kv, qv, att, hid, oacc,
            state, sx, snd, rcv, stg, pri,
            load_sem, own_send, own_recv, recv, relay_recv, relay_send, send_sem,
-           st_send, st_recv, h_send, h_recv, out_sem):
+           st_send, st_recv, h_send, h_recv):
     s = lax.axis_index("seq")
     y = lax.axis_index("tp")
     x, z, c = s // 16, (s // 2) % 8, s % 2
@@ -196,20 +196,28 @@
     def relay(g, column, ref):
         rcopy(ref, ref, relay_send.at[g, column], relay_recv.at[g, column], sib).start()
 
+    def own_arrived(g):
+        i0, n, _ = GROUPS[g]
+        ref = buf.at[pl.ds(i0, n), x, z, 1 - c]
+        rcopy(ref, ref, own_send.at[g], own_recv.at[g], sib).wait_recv()
+
     def event_a(g, slot):
         pc = functools.partial(piece, g, rows=(0, GROUPS[g][2]))
         chain = lambda k, hop, way: 4 + (k * 4 + hop) * 2 + way
         columns = (x, xm, xp, x2)
         if slot < 3:
             k = slot + 1
-            ref = pc(columns[k], z)
             if slot >= 0:
-                arrived(g, ref, slot)
-            else:
-                for o, where in enumerate(("xp", "xm", "x2")):
-                    send(g, 0, ref, o, where)
-            send(g, 1, ref, chain(k, 0, 0), "zp")
-            send(g, 1, ref, chain(k, 0, 1), "zm")
+                arrived(g, pc(columns[k], z), slot)
+            for half in ((0, 1) if (g, slot) == (0, -1) else (None,)):
+                ref = pc(columns[k], z, half=half)
+                if slot < 0:
+                    if half != 0:
+                        own_arrived(g)
+                    for o, where in enumerate(("xp", "xm", "x2")):
+                        send(g, 0, ref, o, where)
+                send(g, 1, ref, chain(k, 0, 0), "zp")
+                send(g, 1, ref, chain(k, 0, 1), "zm")
             if slot >= 0:
                 relay(g, k, ref)
             return
@@ -233,9 +241,14 @@
             send(g, 1, ref, 9 + 4 * k, "xm")
 
         if slot < 0:
-            send(g, 0, pc(x, z), 0, "zp")
-            send(g, 0, pc(x, z), 1, "zm")
-            across(0)
+            for half in ((1, 0) if g == 0 else (None,)):
+                if half != 1:
+                    own_arrived(g)
+                ref = pc(x, z, half=half)
+                send(g, 0, ref, 0, "zp")
+                send(g, 0, ref, 1, "zm")
+                send(g, 1, ref, 8, "xp")
+                send(g, 1, ref, 9, "xm")
         elif slot < 6:
             ref = pc(x, (z + 8 + zs[slot + 1]) % NZ)
             arrived(g, ref, slot)
@@ -263,10 +276,6 @@
 
     def events(core, todo, seen):
         for g, slot in todo:
-            if slot < 0:
-                i0, n, _ = GROUPS[g]
-                ref = buf.at[pl.ds(i0, n), x, z, 1 - c]
-                rcopy(ref, ref, own_send.at[g], own_recv.at[g], sib).wait_recv()
             if core == 0:
                 event_a(g, slot)
             else:
@@ -408,18 +417,23 @@
         hcopy(y2, r, 0, 64, 2).wait_recv()
         hcopy(y2, r, 64, 64, 3).wait_recv()
 
-    def out_part(py, first, last):
+    def out_part(py, first):
         for j in range(6):
             cols = pl.ds(F * j, F)
             w = buf[4, py, :, :, 16 * j:16 * (j + 1), :].reshape(F, F)
             part = jnp.dot(hid[py], w, preferred_element_type=F32)
             if first:
                 oacc[:, cols] = part
-            elif not last:
+            else:
                 oacc[:, cols] += part
-            else:
-                outv[:, cols] = (oacc[:, cols] + part).astype(BF)
-                pltpu.make_async_copy(outv.at[:, cols], out_hbm.at[:, cols], out_sem.at[j]).start()
+
+    def out_last(lo, n):
+        rows = pl.ds(lo, n)
+        for j in range(6):
+            cols = pl.ds(F * j, F)
+            w = buf[4, y2, :, :, 16 * j:16 * (j + 1), :].reshape(F, F)
+            part = jnp.dot(hid[y2, rows, :], w, preferred_element_type=F32)
+            out_ref[rows, cols] = (oacc[rows, cols] + part).astype(BF)
 
     def finish_k():
         kv[0] = silu(acc[0]).astype(BF)
@@ -474,10 +488,13 @@
             if n == 0:
                 for k in range(NX):
                     weights(3, k)
-            if n == 3:
-                for r in range(4):
-                    far(r)
-            out_part((y, ym, yp, y2)[n], n == 0, n == 3)
+            if n < 3:
+                out_part((y, ym, yp)[n], n == 0)
+            else:
+                for half in range(2):
+                    far(2 * half)
+                    far(2 * half + 1)
+                    out_last(256 * half, 256)
 
     seen = (set(), set())
     for name, *todo in PLAN:
@@ -501,10 +518,6 @@
         hcopy(y, r, 0, 128, 1).wait_send()
         hcopy(ym, r, 0, 64, 2).wait_send()
         hcopy(yp, r, 64, 64, 3).wait_send()
-    for j in range(6):
-        cols = pl.ds(F * j, F)
-        pltpu.make_async_copy(outv.at[:, cols], out_hbm.at[:, cols], out_sem.at[j]).wait()
-
 
 def shards(inputs, proj_weight, decay_codes, norm_gain, out_weight):
     vmem = pltpu.VMEM
@@ -517,7 +530,7 @@
         kernel,
         out_shape=jax.ShapeDtypeStruct((T, 1536), BF),
         in_specs=[hbm] * 5,
-        out_specs=pl.BlockSpec(memory_space=pl.ANY),
+        out_specs=pl.BlockSpec(memory_space=vmem),
         scratch_shapes=[
             pltpu.SMEM((2,), jnp.int32),
             vmem((1, F), F32),
@@ -530,7 +543,6 @@
             vmem((T, F), F32),
             vmem((NY, T, F), BF),
             vmem((T, 1536), F32),
-            vmem((T, 1536), BF),
             vmem((2, HD, HD), F32),
             vmem((HD, HD), F32),
             vmem((3, HD, HD), BF),
@@ -548,7 +560,6 @@
             dma((4, 3)),
             dma((4, 4)),
             dma((4, 4)),
-            dma((6,)),
         ],
         compiler_params=pltpu.CompilerParams(collective_id=0, has_side_effects=True, vmem_limit_bytes=52 * 2 ** 20),
         name="lightning",

time: 83 us -> 80.6 us (0.971)
  Pallas kernels: 81.1 us -> 79.4 us
    pallas_call x1, Pallas kernels: 81.1 us -> 79.4 us  [shards(): pl.pallas_call(kernel, out_shape=jax.ShapeDtypeStruct((T, 1536), BF), in_...]
where the time goes in v4:
time: 80.6 us; the launch traced here: 80.5 us
  Pallas kernels  79.4 us (99%)
  local copies, waits for them, and re-layouts  1.15 us (1%)
    pallas_call x1, Pallas kernels, shards(): pl.pallas_call(kernel, out_shape=jax.ShapeDtypeStruct((T, 1536), BF), in_...  79.4 us

profile of v4, /device:TPU:1, one launch (start us, length us, event | category | flops | bytes accessed | tf_op | source)
XLA Modules:
  0.0 80.5 jit_solution(12317892818665596737)
XLA Ops:
  0.0 79.4 %lightning.1 = bf16[512,1536]{1,0:T(8,128)(2,1)S(1)} custom-call(bf16[512,6144]{1,0:T(8,128)(2,1)} %x_hbm.1, bf16[4,96,256]{2,1,0:T(8,128)(2,1)} %wp_hbm.1, s32[2]{0:T(128)} %codes_hbm.1, f32[1,256]{1,0:T(1,128)} %bitcast.1, bf16[16,1536]{1,0:T(8,128)(2,1)} %wo_hbm.1), custom_call_target="tpu_custom_call" | custom-call | tf_op jit(solution)/shard_map/lightning/pallas_call | solution.py:529
  79.4 1.1 %copy.7 = bf16[512,1536]{1,0:T(8,128)(2,1)} copy(bf16[512,1536]{1,0:T(8,128)(2,1)S(1)} %lightning.1) | data formatting | bytes 3145728

commit v5 on v4

--- a/solution.py
+++ b/solution.py
@@ -162,16 +162,20 @@
         ref = buf.at[pl.ds(i0, n), x, z, c]
         return rcopy(ref, ref, own_send.at[g], own_recv.at[g], sib)
 
-    for g in range(len(GROUPS)):
+    def share(g):
         for copy in loads[g]:
             copy.wait()
         own_copy(g).start()
 
-    for copy in small:
-        copy.wait()
+    share(0)
+
     pos = lambda shape, dim: lax.broadcasted_iota(jnp.int32, shape, dim).astype(F32)
-    log_decay = [jnp.log1p(-(jnp.full((1, HD), codes[h], jnp.int32).astype(F32)) * 1e-06) for h in range(2)]
-    ld_mine = jnp.where(c == 0, log_decay[0], log_decay[1])
+    log_decay = []
+
+    def read_decays():
+        for copy in small:
+            copy.wait()
+        log_decay.extend([jnp.log1p(-(jnp.full((1, HD), codes[h], jnp.int32).astype(F32)) * 1e-06) for h in range(2)])
 
     def table(r, carry):
         row = pos((64, T), 0) + (r * 64).astype(F32)
@@ -332,7 +336,7 @@
             kt = (kv[0, :, cols].astype(F32) * tail).astype(BF)
             state[h] = lax.dot_general(kt, kv[1, :, cols], (((0,), (0,)), ((), ())), preferred_element_type=F32)
 
-    whole = lambda n: jnp.exp((n * T) * ld_mine)
+    whole = lambda n: jnp.exp((n * T) * jnp.where(c == 0, log_decay[0], log_decay[1]))
 
     def scan_open():
         rcopy(state.at[1 - c], sx, st_send.at[0, 0], st_recv.at[0, 0], sib).start()
@@ -453,6 +457,9 @@
         kind, n = name.rstrip("0123"), name[-1]
         n = int(n) if n.isdigit() else None
         if kind == "table":
+            for g in range(1, len(GROUPS)):
+                share(g)
+            read_decays()
             lax.fori_loop(0, T // 64, table, 0)
         elif kind in "KVQG":
             item = "KVQG".index(kind)

time: 80.6 us -> 80.6 us (level)
  no operation moved by 1% of the time
where the time goes in v5:
time: 80.6 us; the launch traced here: 80.5 us
  Pallas kernels  79.3 us (98%)
  local copies, waits for them, and re-layouts  1.15 us (1%)
    pallas_call x1, Pallas kernels, shards(): pl.pallas_call(kernel, out_shape=jax.ShapeDtypeStruct((T, 1536), BF), in_...  79.3 us

profile of v5, /device:TPU:1, one launch (start us, length us, event | category | flops | bytes accessed | tf_op | source)
XLA Modules:
  0.0 80.5 jit_solution(7264506198255209364)
XLA Ops:
  0.0 79.3 %lightning.1 = bf16[512,1536]{1,0:T(8,128)(2,1)S(1)} custom-call(bf16[512,6144]{1,0:T(8,128)(2,1)} %x_hbm.1, bf16[4,96,256]{2,1,0:T(8,128)(2,1)} %wp_hbm.1, s32[2]{0:T(128)} %codes_hbm.1, f32[1,256]{1,0:T(1,128)} %bitcast.1, bf16[16,1536]{1,0:T(8,128)(2,1)} %wo_hbm.1), custom_call_target="tpu_custom_call" | custom-call | tf_op jit(solution)/shard_map/lightning/pallas_call | solution.py:536
  79.3 1.1 %copy.7 = bf16[512,1536]{1,0:T(8,128)(2,1)} copy(bf16[512,1536]{1,0:T(8,128)(2,1)S(1)} %lightning.1) | data formatting | bytes 3145728
